TPU v7x, 32 devices: a whole 2x2x4 slice. The times are simulated.
32 devices in a mesh: groups: 2 (over x), row: 2 (over core), col: 8 (over z, y).
Axes of the slice: x: 2, y: 2, z: 4, core: 2. Of those that a mesh axis runs over, the one named last changes fastest.
Arguments:
- pair: bfloat16 [1280, 640, 128], P(('groups', 'col'), 'row'), parts along dimension 0, may hold values from -6 to 6
- token_mask: int32 [1280], P('groups'), parts along dimension 0, may hold values 0 or 1
- start_gain: float32 [128], replicated, may hold values from 0.25 to 1.75
- start_head_gain: float32 [128], replicated, may hold values from 0.25 to 1.75
- start_in: bfloat16 [128, 512], replicated, may hold values from -0.5 to 0.5
- start_out: bfloat16 [128, 128], replicated, may hold values from -0.5 to 0.5
- end_gain: float32 [128], replicated, may hold values from 0.25 to 1.75
- end_head_gain: float32 [128], replicated, may hold values from 0.25 to 1.75
- end_in: bfloat16 [128, 512], replicated, may hold values from -0.5 to 0.5
- end_out: bfloat16 [128, 128], replicated, may hold values from -0.5 to 0.5
- trans_gain: float32 [128], replicated, may hold values from 0.25 to 1.75
- trans_in: bfloat16 [128, 1024], replicated, may hold values from -0.5 to 0.5
- trans_out: bfloat16 [512, 128], replicated, may hold values from -0.25 to 0.25
Outputs:
- update_start: bfloat16 [1280, 640, 128], P(('groups', 'col'), 'row'), parts along dimension 0
- update_end: bfloat16 [1280, 640, 128], P(('groups', 'col'), 'row'), parts along dimension 0
- update_trans: bfloat16 [1280, 640, 128], P(('groups', 'col'), 'row'), parts along dimension 0
There are 2 independent parts, one for each index of `groups`. A program takes and returns all parts, laid end to end along the dimension named above; an argument that names none is the same for every part. Nothing has to cross between parts.
Inputs may be any that keep to these rules, and one draw needn't show every extreme that they name: `token_mask`: 1 marks a valid token of the complex, 0 a padded one.
All inputs are finite; a program needn't handle non-finite values.
Results may differ from a plain program's by a relative error of at most 0.018.
Values may be sent and summed in bfloat16 or wider, within the bound.
A program may use at most 192 MiB of HBM per device.

v0:
```python
import functools
import math

import jax
import jax.numpy as jnp
from jax import lax
from jax.experimental import pallas as pl
from jax.experimental.pallas import tpu as pltpu
from jax.sharding import PartitionSpec as P

HEADS = 4
EPSILON = 1e-05
F32 = jnp.float32
BF16 = jnp.bfloat16
CHUNKS = 4
VMEM_BYTES = 52 * 1024 * 1024


def mean_matrix(width):
    return jnp.full((width, width), 1.0 / width, BF16)


def center_matrix(width, copies):
    rows = lax.broadcasted_iota(jnp.int32, (width, width), 0)
    cols = lax.broadcasted_iota(jnp.int32, (width, width), 1)
    once = jnp.where(rows == cols, 1.0 - 1.0 / width, -1.0 / width)
    return jnp.concatenate([once] * copies, axis=0).astype(BF16)


def layer_norm(parts, scales):
    width = parts[0].shape[-1]
    joined = parts[0] if len(parts) == 1 else jnp.concatenate(parts, axis=1)
    centered = matmul(joined, center_matrix(width, len(parts)))
    variance = matmul((centered * centered).astype(BF16), mean_matrix(width))
    return (centered * lax.rsqrt(variance + EPSILON) * scales).astype(BF16)


def feature(values):
    return jnp.maximum(values + 1.0, jnp.exp(jnp.minimum(values, 0.0)))


def sigmoid(values):
    return 0.5 + 0.5 * jnp.tanh(0.5 * values)


def matmul(left, right):
    return jnp.dot(left, right, preferred_element_type=F32)


def same_head(width):
    depth = width // HEADS
    rows = lax.broadcasted_iota(jnp.int32, (width, width), 0) // depth
    cols = lax.broadcasted_iota(jnp.int32, (width, width), 1) // depth
    return rows == cols


def outer_compact(keys, values):
    width = keys.shape[-1]
    depth = width // HEADS
    full = lax.dot_general(keys, values, (((0,), (0,)), ((), ())), preferred_element_type=F32)
    head = lax.broadcasted_iota(jnp.int32, (depth, width), 1) // depth
    result = full[:depth]
    for h in range(1, HEADS):
        result = jnp.where(head == h, full[h * depth : (h + 1) * depth], result)
    return result


def expand(state, same):
    tiled = jnp.concatenate([state.astype(F32)] * HEADS, axis=0)
    return jnp.where(same, tiled, 0.0).astype(BF16)


def query_gate(w):
    width = w.shape[0]
    return jnp.concatenate([w[:, :width], w[:, 3 * width :]], axis=1)


def head_norm(numer, denom, gate, head_gain):
    attended = numer * pl.reciprocal(jnp.maximum(denom, 1.0))
    square = matmul((attended * attended).astype(BF16), mean_matrix(numer.shape[-1]))
    scale = lax.rsqrt(square + EPSILON)
    return (attended * scale * head_gain * sigmoid(gate)).astype(BF16)


def row_state_kernel(row_valid, pair, col_mask, gain, w, out):
    count, cols, width = pair.shape
    depth = width // HEADS
    base = pl.program_id(0) * count
    normed = layer_norm([pair[...].reshape(count * cols, width)], gain[...])
    project = matmul(normed, w[:, width : 3 * width])
    keys = feature(project[:, :width]).reshape(count, cols, width) * col_mask[...][None]
    keys = keys.astype(BF16)
    values = project[:, width:].reshape(count, cols, width).astype(BF16)
    for i in range(count):
        valid = row_valid[base + i]
        out[i, 0:depth, :] = (outer_compact(keys[i], values[i]) * valid).astype(BF16)
        total = jnp.sum(keys[i].astype(F32), axis=0, keepdims=True) * valid
        out[i, depth : depth + 16, :] = jnp.broadcast_to(total, (16, width)).astype(BF16)


def start_kernel(row_size, pair, *rest):
    states, rest = rest[:row_size], rest[row_size:]
    gain, head_gain, w, w_out, end_gain = rest[:5]
    update, normed_end = rest[-2:]
    count, cols, width = pair.shape
    depth = width // HEADS
    same = same_head(width)
    ones = same.astype(F32).astype(BF16)
    field = pair[...].reshape(count * cols, width)
    project = matmul(layer_norm([field], gain[...]), query_gate(w[...]))
    queries = feature(project[:, :width]).reshape(count, cols, width).astype(BF16)
    numer, weighted = [], []
    for i in range(count):
        state = sum(s[i, 0:depth, :].astype(F32) for s in states)
        totals = sum(s[i, depth : depth + 16, :].astype(F32) for s in states)
        numer.append(matmul(queries[i], expand(state, same)))
        weighted.append(queries[i].astype(F32) * totals[0:1])
    denom = matmul(jnp.concatenate(weighted, axis=0).astype(BF16), ones)
    scaled = head_norm(
        jnp.concatenate(numer, axis=0), denom, project[:, width:], head_gain[...]
    )
    result = matmul(scaled, w_out[...]).astype(BF16)
    update[...] = result.reshape(count, cols, width)
    normed_end[...] = layer_norm([field, result], end_gain[...]).reshape(count, cols, width)


def columns_first(normed, scratch):
    rows, count, width = normed.shape
    scratch[...] = normed[...].astype(F32).reshape(rows * count, width)
    return jnp.concatenate(
        [scratch[pl.ds(j, rows, stride=count), :] for j in range(count)], axis=0
    ).astype(BF16)


def column_state_kernel(first, col_valid, normed, row_mask, w, out, scratch):
    rows, count, width = normed.shape
    depth = width // HEADS
    base = first + pl.program_id(0) * count
    project = matmul(columns_first(normed, scratch), w[:, width : 3 * width])
    keys = feature(project[:, :width]).reshape(count, rows, width) * row_mask[...][None]
    keys = keys.astype(BF16)
    values = project[:, width:].reshape(count, rows, width).astype(BF16)
    totals = []
    for j in range(count):
        valid = col_valid[base + j]
        out[0, j * depth : (j + 1) * depth, :] = (
            outer_compact(keys[j], values[j]) * valid
        ).astype(BF16)
        totals.append(jnp.sum(keys[j].astype(F32), axis=0, keepdims=True) * valid)
    out[0, count * depth : count * (depth + 1), :] = jnp.concatenate(totals, axis=0).astype(BF16)


def end_kernel(
    normed, pair, update_start, state, head_gain, w, w_out, trans_gain, trans_in, trans_out, *rest
):
    update_end, update_trans, scratch, turned = rest[-4:]
    rows, count, width = normed.shape
    depth = width // HEADS
    hidden = trans_out.shape[0]
    same = same_head(width)
    ones = same.astype(F32).astype(BF16)
    project = matmul(columns_first(normed, scratch), query_gate(w[...]))
    queries = feature(project[:, :width]).reshape(count, rows, width).astype(BF16)
    totals = state[0, count * depth : count * (depth + 1), :].astype(F32)
    numer, weighted = [], []
    for j in range(count):
        numer.append(matmul(queries[j], expand(state[0, j * depth : (j + 1) * depth, :], same)))
        weighted.append(queries[j].astype(F32) * totals[j : j + 1])
    denom = matmul(jnp.concatenate(weighted, axis=0).astype(BF16), ones)
    scaled = head_norm(
        jnp.concatenate(numer, axis=0), denom, project[:, width:], head_gain[...]
    )
    result = matmul(scaled, w_out[...])
    for j in range(count):
        turned[pl.ds(j, rows, stride=count), :] = result[j * rows : (j + 1) * rows]
    ended = turned[...].astype(BF16)
    update_end[...] = ended.reshape(rows, count, width)
    parts = [part[...].reshape(rows * count, width) for part in (pair, update_start)]
    y = layer_norm(parts + [ended], trans_gain[...])
    step = math.gcd(hidden, 256)
    moved = jnp.zeros((rows * count, width), F32)
    for at in range(0, hidden, step):
        gate = (0.5 * matmul(y, trans_in[:, at : at + step])).astype(BF16)
        up = matmul(y, trans_in[:, hidden + at : hidden + at + step]).astype(BF16)
        h = (gate + gate * jnp.tanh(gate)) * up
        moved = moved + matmul(h, trans_out[at : at + step, :])
    update_trans[...] = moved.astype(BF16).reshape(rows, count, width)


def exchange_sum(values, size, bits, done):
    me = lax.axis_index("col")
    for bit in bits:
        yield values
        half = values.shape[0] // 2
        mine = (me >> bit) & 1
        pairs = [(d, d ^ (1 << bit)) for d in range(size)]
        sent = lax.dynamic_slice_in_dim(values, (1 - mine) * half, half)
        kept = lax.dynamic_slice_in_dim(values, mine * half, half)
        got = lax.ppermute(sent, "col", pairs)
        values = (kept.astype(F32) + got.astype(F32)).astype(BF16)
    for bit in reversed(bits):
        yield values
        mine = (me >> bit) & 1
        pairs = [(d, d ^ (1 << bit)) for d in range(size)]
        got = lax.ppermute(values, "col", pairs)
        values = jnp.where(
            mine == 1,
            jnp.concatenate([got, values], axis=0),
            jnp.concatenate([values, got], axis=0),
        )
    done.append(values)


def params():
    return pltpu.CompilerParams(vmem_limit_bytes=VMEM_BYTES, dimension_semantics=("arbitrary",))


def cost(flops):
    return pl.CostEstimate(flops=int(flops), bytes_accessed=1 << 20, transcendentals=0)


def shards(
    size,
    row_size,
    pair,
    token_mask,
    start_gain,
    start_head_gain,
    start_in,
    start_out,
    end_gain,
    end_head_gain,
    end_in,
    end_out,
    trans_gain,
    trans_in,
    trans_out,
):
    rows, cols, width = pair.shape
    depth = width // HEADS
    valid = token_mask.astype(F32)
    row_valid = lax.dynamic_slice_in_dim(valid, lax.axis_index("col") * rows, rows)
    col_valid = lax.dynamic_slice_in_dim(valid, lax.axis_index("row") * cols, cols)
    row_mask = jnp.broadcast_to(row_valid[:, None], (rows, width))
    col_mask = jnp.broadcast_to(col_valid[:, None], (cols, width))
    gains = [
        g.reshape(1, width) for g in (start_gain, start_head_gain, end_gain, end_head_gain, trans_gain)
    ]
    start_gain, start_head_gain, end_gain, end_head_gain, trans_gain = gains
    smem = pl.BlockSpec(memory_space=pltpu.SMEM)
    anywhere = pl.BlockSpec(memory_space=pl.ANY)

    def whole(array):
        return pl.BlockSpec(array.shape, lambda g: (0,) * array.ndim)

    group = math.gcd(rows, 8)
    packed = depth + 16
    row_state = pl.pallas_call(
        row_state_kernel,
        grid=(rows // group,),
        in_specs=[
            smem,
            pl.BlockSpec((group, cols, width), lambda g: (g, 0, 0)),
            whole(col_mask),
            whole(start_gain),
            whole(start_in),
        ],
        out_specs=pl.BlockSpec((group, packed, width), lambda g: (g, 0, 0)),
        out_shape=jax.ShapeDtypeStruct((rows, packed, width), BF16),
        compiler_params=params(),
        cost_estimate=cost(2e10),
        name="row_state",
    )(row_valid, pair, col_mask, start_gain, start_in)
    row_states = [row_state] + [
        lax.ppermute(row_state, "row", [(d, (d + k) % row_size) for d in range(row_size)])
        for k in range(1, row_size)
    ]

    tile = 16
    chunks = math.gcd(cols // tile, CHUNKS)
    part = cols // chunks
    tiles = part // tile
    block = tile * (depth + 1)
    pad = -(tiles * block) % (16 * size)
    bits = list(range(size.bit_length() - 1))
    full = jax.ShapeDtypeStruct(pair.shape, BF16)
    flying = []

    def advance(small):
        for steps in list(flying):
            ready = next(steps, None)
            if ready is None:
                flying.remove(steps)
            else:
                small, _ = lax.optimization_barrier((small, ready))
        return small

    group = math.gcd(rows, 16)
    update_start = None
    normed_parts, column_states = [], []
    for chunk in range(chunks):
        extra = [] if update_start is None else [update_start]
        pair_block = pl.BlockSpec((group, part, width), lambda g, c=chunk: (g, c, 0))
        update_start, normed = pl.pallas_call(
            functools.partial(start_kernel, row_size),
            grid=(rows // group,),
            in_specs=[pair_block]
            + [pl.BlockSpec((group, packed, width), lambda g: (g, 0, 0))] * row_size
            + [
                whole(start_gain),
                whole(start_head_gain),
                whole(start_in),
                whole(start_out),
                whole(end_gain),
            ]
            + [anywhere] * len(extra),
            out_specs=[pair_block, pl.BlockSpec((group, part, width), lambda g: (g, 0, 0))],
            out_shape=[full, jax.ShapeDtypeStruct((rows, part, width), BF16)],
            input_output_aliases={6 + row_size: 0} if extra else {},
            compiler_params=params(),
            cost_estimate=cost(1e10),
            name="start_finish",
        )(
            pair,
            *row_states,
            advance(start_gain),
            start_head_gain,
            start_in,
            start_out,
            end_gain,
            *extra,
        )
        normed_parts.append(normed)
        state = pl.pallas_call(
            functools.partial(column_state_kernel, chunk * part),
            grid=(tiles,),
            in_specs=[
                smem,
                pl.BlockSpec((rows, tile, width), lambda g: (0, g, 0)),
                whole(row_mask),
                whole(end_in),
            ],
            out_specs=pl.BlockSpec((1, block, width), lambda g: (g, 0, 0)),
            out_shape=jax.ShapeDtypeStruct((tiles, block, width), BF16),
            scratch_shapes=[pltpu.VMEM((rows * tile, width), F32)],
            compiler_params=params(),
            cost_estimate=cost(6e9),
            name="column_state",
        )(col_valid, normed, advance(row_mask), end_in)
        order = bits if chunk % 2 == 0 else bits[1:] + bits[:1]
        state = jnp.pad(state.reshape(tiles * block, width), ((0, pad), (0, 0)))
        column_states.append([])
        flying.append(exchange_sum(state, size, order, column_states[-1]))

    outs = []
    for chunk in range(chunks):
        done = 0
        pieces = [(tiles + 1) // 2, tiles // 2] if 2 * chunk < chunks else [tiles]
        for piece in pieces:
            if not piece:
                continue
            small = advance(end_head_gain)
            while not column_states[chunk]:
                small = advance(small)
            state = column_states[chunk][0][: tiles * block].reshape(tiles, block, width)
            pair_block = pl.BlockSpec(
                (rows, tile, width), lambda g, c=chunk * tiles + done: (0, c + g, 0)
            )
            outs = pl.pallas_call(
                end_kernel,
                grid=(piece,),
                in_specs=[
                    pl.BlockSpec((rows, tile, width), lambda g, c=done: (0, c + g, 0)),
                    pair_block,
                    pair_block,
                    pl.BlockSpec((1, block, width), lambda g, c=done: (c + g, 0, 0)),
                    whole(end_head_gain),
                    whole(end_in),
                    whole(end_out),
                    whole(trans_gain),
                    whole(trans_in),
                    whole(trans_out),
                ]
                + [anywhere] * len(outs),
                out_specs=[pair_block, pair_block],
                out_shape=[full, full],
                scratch_shapes=[pltpu.VMEM((rows * tile, width), F32)] * 2,
                input_output_aliases={10: 0, 11: 1} if outs else {},
                compiler_params=params(),
                cost_estimate=cost(1e10),
                name="end_finish",
            )(
                normed_parts[chunk],
                pair,
                update_start,
                state,
                small,
                end_in,
                end_out,
                trans_gain,
                trans_in,
                trans_out,
                *outs,
            )
            done += piece
    return (update_start, outs[0], outs[1])


def solution(mesh):
    field = P(("groups", "col"), "row", None)
    in_specs = (field, P("groups")) + (P(),) * 11
    return jax.shard_map(
        functools.partial(shards, mesh.shape["col"], mesh.shape["row"]),
        mesh=mesh,
        in_specs=in_specs,
        out_specs=(field, field, field),
        check_vma=False,
    )
```

profile of v0, /device:TPU:0, one launch (start us, length us, event | category | flops | bytes accessed | tf_op | source)
XLA Modules:
  0.0 212.3 jit_solution(11090596367249423098)
XLA Ops:
  0.6 0.7 convert_element_type.116
  1.6 0.9 copy-done.1
  2.5 0.7 copy-done.7
  3.2 15.0 %row_state.1.rest_0_ = bf16[80,48,128]{2,1,0:T(8,128)(2,1)S(1)} custom-call(f32[80]{0:T(128)S(1)} %dynamic_slice.78.row_valid, bf16[80,320,128]{2,1,0:T(8,128)(2,1)} %pair.21, f32[320,128]{1,0:T(8,128)S(1)} %broadcast_in_dim.4.col_mask, f32[1,128]{1,0:T(1,128)S(1)} %bitcast.27, bf16[128,512]{1,0:T(8,128)(2,1)S(1)} %copy-done.1), custom_call_target="tpu_custom_call" | custom-call | flops 20000000000 | bytes 1048576 | tf_op jit(solution)/shard_map/row_state/pallas_call | solution.py:258
  18.2 0.5 collective-permute-start
  18.7 2.2 %collective-permute-done.rest_1_ = bf16[80,48,128]{2,1,0:T(8,128)(2,1)S(1)} collective-permute-done((bf16[80,48,128]{2,1,0:T(8,128)(2,1)S(1)}, bf16[80,48,128]{2,1,0:T(8,128)(2,1)S(1)}, u32[]{:S(2)}, u32[]{:S(2)}) %collective-permute-start) | collective-permute-done | bytes 983072 | tf_op jit(solution)/shard_map/ppermute | solution.py:275
  20.9 0.9 copy-done.13
  21.9 10.0 %start_finish.4 = (bf16[80,320,128]{2,1,0:T(8,128)(2,1)}, bf16[80,80,128]{2,1,0:T(8,128)(2,1)}) custom-call(bf16[80,320,128]{2,1,0:T(8,128)(2,1)} %pair.21, bf16[80,48,128]{2,1,0:T(8,128)(2,1)S(1)} %row_state.1.rest_0_, bf16[80,48,128]{2,1,0:T(8,128)(2,1)} %copy-done.13, f32[1,128]{1,0:T(1,128)S(1)} %bitcast.28, f32[1,128]{1,0:T(1,128)S(1)} %bitcast.32, ...), custom_call_target="tpu_custom_call" | custom-call | flops 10000000000 | bytes 1048576 | tf_op jit(solution)/shard_map/start_finish/pallas_call | solution.py:304
  31.9 5.2 %column_state.4 = bf16[5,528,128]{2,1,0:T(8,128)(2,1)S(1)} custom-call(f32[320]{0:T(512)S(1)} %dynamic_slice.79.col_valid, bf16[80,80,128]{2,1,0:T(8,128)(2,1)} %get-tuple-element.47.normed, f32[80,128]{1,0:T(8,128)S(1)} %broadcast_in_dim.5.row_mask, bf16[128,512]{1,0:T(8,128)(2,1)S(1)} %copy-done.3), custom_call_target="tpu_custom_call" | custom-call | flops 6000000000 | bytes 1048576 | tf_op jit(solution)/shard_map/column_state/pallas_call | solution.py:334
  37.2 3.0 %collective-permute-start.1 = (bf16[1344,128]{1,0:T(8,128)(2,1)S(1)}, bf16[1344,128]{1,0:T(8,128)(2,1)S(1)}, u32[]{:S(2)}, u32[]{:S(2)}) collective-permute-start(bf16[1344,128]{1,0:T(8,128)(2,1)S(1)} %constant_dynamic-slice_fusion.11), channel_id=1, source_target_pairs={{0,1},{1,0},{2,3},{3,2},{4,5},{5,4},{6,7},{7,6},{8,9},{9,8},{10,11... | collective-permute-start | bytes 1032200 | tf_op jit(solution)/shard_map/ppermute | solution.py:199
  40.1 9.9 %start_finish.5 = (bf16[80,320,128]{2,1,0:T(8,128)(2,1)}, bf16[80,80,128]{2,1,0:T(8,128)(2,1)}) custom-call(bf16[80,320,128]{2,1,0:T(8,128)(2,1)} %pair.21, bf16[80,48,128]{2,1,0:T(8,128)(2,1)S(1)} %row_state.1.rest_0_, bf16[80,48,128]{2,1,0:T(8,128)(2,1)} %copy-done.13, f32[1,128]{1,0:T(1,128)S(1)} %bitcast.29, ...), custom_call_target="tpu_custom_call", output_to_operand_aliasing={{0}: (8, {})} | custom-call | flops 10000000000 | bytes 1048576 | tf_op jit(solution)/shard_map/start_finish/pallas_call | solution.py:304
  50.1 1.6 collective-permute-start.2
  51.8 5.1 %column_state.5 = bf16[5,528,128]{2,1,0:T(8,128)(2,1)S(1)} custom-call(f32[320]{0:T(512)S(1)} %dynamic_slice.79.col_valid, bf16[80,80,128]{2,1,0:T(8,128)(2,1)} %get-tuple-element.51.normed, f32[80,128]{1,0:T(8,128)S(1)} %broadcast_in_dim.5.row_mask, bf16[128,512]{1,0:T(8,128)(2,1)S(1)} %copy-done.3), custom_call_target="tpu_custom_call" | custom-call | flops 6000000000 | bytes 1048576 | tf_op jit(solution)/shard_map/column_state/pallas_call | solution.py:334
  57.0 2.7 %collective-permute-start.3 = (bf16[336,128]{1,0:T(8,128)(2,1)S(1)}, bf16[336,128]{1,0:T(8,128)(2,1)S(1)}, u32[]{:S(2)}, u32[]{:S(2)}) collective-permute-start(bf16[336,128]{1,0:T(8,128)(2,1)S(1)} %constant_dynamic-slice_fusion.9), channel_id=1, source_target_pairs={{0,4},{1,5},{2,6},{3,7},{4,0},{5,1},{6,2},{7,3},{8,12},{9,13},{10,... | collective-permute-start | bytes 258056 | tf_op jit(solution)/shard_map/ppermute | solution.py:199
  59.7 1.0 collective-permute-start.5
  60.8 3.0 %collective-permute-done.3 = bf16[336,128]{1,0:T(8,128)(2,1)S(1)} collective-permute-done((bf16[336,128]{1,0:T(8,128)(2,1)S(1)}, bf16[336,128]{1,0:T(8,128)(2,1)S(1)}, u32[]{:S(2)}, u32[]{:S(2)}) %collective-permute-start.3) | collective-permute-done | bytes 86048 | tf_op jit(solution)/shard_map/ppermute | solution.py:199
  63.8 2.4 %collective-permute-start.4 = (bf16[336,128]{1,0:T(8,128)(2,1)S(1)}, bf16[336,128]{1,0:T(8,128)(2,1)S(1)}, u32[]{:S(2)}, u32[]{:S(2)}) collective-permute-start(bf16[336,128]{1,0:T(8,128)(2,1)S(1)} %add_convert_fusion.11), channel_id=1, source_target_pairs={{0,4},{1,5},{2,6},{3,7},{4,0},{5,1},{6,2},{7,3},{8,12},{9,13},{10,... | collective-permute-start | bytes 258056 | tf_op jit(solution)/shard_map/ppermute | solution.py:205
  66.1 9.9 %start_finish.6 = (bf16[80,320,128]{2,1,0:T(8,128)(2,1)}, bf16[80,80,128]{2,1,0:T(8,128)(2,1)}) custom-call(bf16[80,320,128]{2,1,0:T(8,128)(2,1)} %pair.21, bf16[80,48,128]{2,1,0:T(8,128)(2,1)S(1)} %row_state.1.rest_0_, bf16[80,48,128]{2,1,0:T(8,128)(2,1)} %copy-done.13, f32[1,128]{1,0:T(1,128)S(1)} %bitcast.30, ...), custom_call_target="tpu_custom_call", output_to_operand_aliasing={{0}: (8, {})} | custom-call | flops 10000000000 | bytes 1048576 | tf_op jit(solution)/shard_map/start_finish/pallas_call | solution.py:304
  76.1 0.5 collective-permute-start.7
  76.7 0.8 collective-permute-start.6
  77.6 5.1 %column_state.6 = bf16[5,528,128]{2,1,0:T(8,128)(2,1)S(1)} custom-call(f32[320]{0:T(512)S(1)} %dynamic_slice.79.col_valid, bf16[80,80,128]{2,1,0:T(8,128)(2,1)} %get-tuple-element.57.normed, f32[80,128]{1,0:T(8,128)S(1)} %broadcast_in_dim.5.row_mask, bf16[128,512]{1,0:T(8,128)(2,1)S(1)} %copy-done.3), custom_call_target="tpu_custom_call" | custom-call | flops 6000000000 | bytes 1048576 | tf_op jit(solution)/shard_map/column_state/pallas_call | solution.py:334
  82.8 0.6 collective-permute-start.9
  83.3 2.2 %collective-permute-done.6 = bf16[672,128]{1,0:T(8,128)(2,1)S(1)} collective-permute-done((bf16[672,128]{1,0:T(8,128)(2,1)S(1)}, bf16[672,128]{1,0:T(8,128)(2,1)S(1)}, u32[]{:S(2)}, u32[]{:S(2)}) %collective-permute-start.6) | collective-permute-done | bytes 172064 | tf_op jit(solution)/shard_map/ppermute | solution.py:199
  85.9 1.9 collective-permute-start.24
  87.8 7.9 %collective-permute-done.8 = bf16[336,128]{1,0:T(8,128)(2,1)S(1)} collective-permute-done((bf16[336,128]{1,0:T(8,128)(2,1)S(1)}, bf16[336,128]{1,0:T(8,128)(2,1)S(1)}, u32[]{:S(2)}, u32[]{:S(2)}) %collective-permute-start.8) | collective-permute-done | bytes 86048 | tf_op jit(solution)/shard_map/ppermute | solution.py:199
  95.7 0.6 collective-permute-start.21
  96.3 9.9 %start_finish.7 = (bf16[80,320,128]{2,1,0:T(8,128)(2,1)}, bf16[80,80,128]{2,1,0:T(8,128)(2,1)}) custom-call(bf16[80,320,128]{2,1,0:T(8,128)(2,1)} %pair.21, bf16[80,48,128]{2,1,0:T(8,128)(2,1)S(1)} %row_state.1.rest_0_, bf16[80,48,128]{2,1,0:T(8,128)(2,1)} %copy-done.13, f32[1,128]{1,0:T(1,128)S(1)} %bitcast.31, ...), custom_call_target="tpu_custom_call", output_to_operand_aliasing={{0}: (8, {})} | custom-call | flops 10000000000 | bytes 1048576 | tf_op jit(solution)/shard_map/start_finish/pallas_call | solution.py:304
  106.2 2.2 %collective-permute-start.22 = (bf16[672,128]{1,0:T(8,128)(2,1)S(1)}, bf16[672,128]{1,0:T(8,128)(2,1)S(1)}, u32[]{:S(2)}, u32[]{:S(2)}) collective-permute-start(bf16[672,128]{1,0:T(8,128)(2,1)S(1)} %maximum_select_fusion.7), channel_id=1, source_target_pairs={{0,4},{1,5},{2,6},{3,7},{4,0},{5,1},{6,2},{7,3},{8,12},{9,13},{10,... | collective-permute-start | bytes 516104 | tf_op jit(solution)/shard_map/ppermute | solution.py:205
  108.6 1.4 collective-permute-start.16
  110.0 5.1 %column_state.7 = bf16[5,528,128]{2,1,0:T(8,128)(2,1)S(1)} custom-call(f32[320]{0:T(512)S(1)} %dynamic_slice.79.col_valid, bf16[80,80,128]{2,1,0:T(8,128)(2,1)} %get-tuple-element.63.normed, f32[80,128]{1,0:T(8,128)S(1)} %broadcast_in_dim.5.row_mask, bf16[128,512]{1,0:T(8,128)(2,1)S(1)} %copy-done.3), custom_call_target="tpu_custom_call" | custom-call | flops 6000000000 | bytes 1048576 | tf_op jit(solution)/shard_map/column_state/pallas_call | solution.py:334
  115.2 0.8 collective-permute-start.10
  116.0 1.6 collective-permute-done.16
  117.6 2.0 collective-permute-start.17
  119.7 1.4 collective-permute-start.23
  121.4 11.2 %end_finish.6 = (bf16[80,320,128]{2,1,0:T(8,128)(2,1)}, bf16[80,320,128]{2,1,0:T(8,128)(2,1)}) custom-call(bf16[80,80,128]{2,1,0:T(8,128)(2,1)} %get-tuple-element.47.normed, bf16[80,320,128]{2,1,0:T(8,128)(2,1)} %pair.21, bf16[80,320,128]{2,1,0:T(8,128)(2,1)} %get-tuple-element.44.update_start, bf16[5,528,128]{2,1,0:T(8,128)(2,1)S(1)} %bitcast.21, ...), custom_call_target="tpu_custom_call" | custom-call | flops 10000000000 | bytes 1048576 | tf_op jit(solution)/shard_map/end_finish/pallas_call | solution.py:369
  132.6 1.6 collective-permute-start.18
  134.3 1.5 collective-permute-start.11
  135.8 5.0 %collective-permute-done.18 = bf16[336,128]{1,0:T(8,128)(2,1)S(1)} collective-permute-done((bf16[336,128]{1,0:T(8,128)(2,1)S(1)}, bf16[336,128]{1,0:T(8,128)(2,1)S(1)}, u32[]{:S(2)}, u32[]{:S(2)}) %collective-permute-start.18) | collective-permute-done | bytes 86048 | tf_op jit(solution)/shard_map/ppermute | solution.py:205
  140.9 8.1 %end_finish.7 = (bf16[80,320,128]{2,1,0:T(8,128)(2,1)}, bf16[80,320,128]{2,1,0:T(8,128)(2,1)}) custom-call(bf16[80,80,128]{2,1,0:T(8,128)(2,1)} %get-tuple-element.47.normed, bf16[80,320,128]{2,1,0:T(8,128)(2,1)} %pair.21, bf16[80,320,128]{2,1,0:T(8,128)(2,1)} %get-tuple-element.44.update_start, ...), custom_call_target="tpu_custom_call", output_to_operand_aliasing={{0}: (10, {}), {1}: (11, {})} | custom-call | flops 10000000000 | bytes 1048576 | tf_op jit(solution)/shard_map/end_finish/pallas_call | solution.py:369
  149.1 1.7 collective-permute-start.12
  151.0 0.4 collective-permute-start.20
  151.6 2.1 collective-permute-done.12
  153.7 1.7 collective-permute-start.13
  155.4 11.2 %end_finish.8 = (bf16[80,320,128]{2,1,0:T(8,128)(2,1)}, bf16[80,320,128]{2,1,0:T(8,128)(2,1)}) custom-call(bf16[80,80,128]{2,1,0:T(8,128)(2,1)} %get-tuple-element.51.normed, bf16[80,320,128]{2,1,0:T(8,128)(2,1)} %pair.21, bf16[80,320,128]{2,1,0:T(8,128)(2,1)} %get-tuple-element.44.update_start, ...), custom_call_target="tpu_custom_call", output_to_operand_aliasing={{0}: (10, {}), {1}: (11, {})} | custom-call | flops 10000000000 | bytes 1048576 | tf_op jit(solution)/shard_map/end_finish/pallas_call | solution.py:369
  166.7 8.3 %end_finish.9 = (bf16[80,320,128]{2,1,0:T(8,128)(2,1)}, bf16[80,320,128]{2,1,0:T(8,128)(2,1)}) custom-call(bf16[80,80,128]{2,1,0:T(8,128)(2,1)} %get-tuple-element.51.normed, bf16[80,320,128]{2,1,0:T(8,128)(2,1)} %pair.21, bf16[80,320,128]{2,1,0:T(8,128)(2,1)} %get-tuple-element.44.update_start, ...), custom_call_target="tpu_custom_call", output_to_operand_aliasing={{0}: (10, {}), {1}: (11, {})} | custom-call | flops 10000000000 | bytes 1048576 | tf_op jit(solution)/shard_map/end_finish/pallas_call | solution.py:369
  175.2 2.0 collective-permute-start.15
  177.4 17.3 %end_finish.10 = (bf16[80,320,128]{2,1,0:T(8,128)(2,1)}, bf16[80,320,128]{2,1,0:T(8,128)(2,1)}) custom-call(bf16[80,80,128]{2,1,0:T(8,128)(2,1)} %get-tuple-element.57.normed, bf16[80,320,128]{2,1,0:T(8,128)(2,1)} %pair.21, bf16[80,320,128]{2,1,0:T(8,128)(2,1)} %get-tuple-element.44.update_start, ...), custom_call_target="tpu_custom_call", output_to_operand_aliasing={{0}: (10, {}), {1}: (11, {})} | custom-call | flops 10000000000 | bytes 1048576 | tf_op jit(solution)/shard_map/end_finish/pallas_call | solution.py:369
  194.9 17.3 %end_finish.11 = (bf16[80,320,128]{2,1,0:T(8,128)(2,1)}, bf16[80,320,128]{2,1,0:T(8,128)(2,1)}) custom-call(bf16[80,80,128]{2,1,0:T(8,128)(2,1)} %get-tuple-element.63.normed, bf16[80,320,128]{2,1,0:T(8,128)(2,1)} %pair.21, bf16[80,320,128]{2,1,0:T(8,128)(2,1)} %get-tuple-element.44.update_start, ...), custom_call_target="tpu_custom_call", output_to_operand_aliasing={{0}: (10, {}), {1}: (11, {})} | custom-call | flops 10000000000 | bytes 1048576 | tf_op jit(solution)/shard_map/end_finish/pallas_call | solution.py:369
  (86 shorter events, 3.1 us)
Async XLA Ops:
  1.6 0.9 copy-start.1
  2.5 0.7 copy-start.7
  3.2 18.7 %copy-start.2 = (bf16[128,512]{1,0:T(8,128)(2,1)S(1)}, bf16[128,512]{1,0:T(8,128)(2,1)}, u32[]{:S(2)}) copy-start(bf16[128,512]{1,0:T(8,128)(2,1)} %rest_4_.7) | copy-start | bytes 393220
  3.2 18.7 %copy-start.5 = (bf16[128,128]{1,0:T(8,128)(2,1)S(1)}, bf16[128,128]{1,0:T(8,128)(2,1)}, u32[]{:S(2)}) copy-start(bf16[128,128]{1,0:T(8,128)(2,1)} %rest_5_.7) | copy-start | bytes 98308
  3.2 18.7 %copy-start.8 = (f32[128]{0:T(128)S(1)}, f32[128]{0:T(128)}, u32[]{:S(2)}) copy-start(f32[128]{0:T(128)} %param.15) | copy-start | bytes 1540
  3.2 18.7 %copy-start.9 = (f32[128]{0:T(128)S(1)}, f32[128]{0:T(128)}, u32[]{:S(2)}) copy-start(f32[128]{0:T(128)} %param.16) | copy-start | bytes 1540
  3.2 18.7 %copy-start.10 = (f32[128]{0:T(128)S(1)}, f32[128]{0:T(128)}, u32[]{:S(2)}) copy-start(f32[128]{0:T(128)} %param.19) | copy-start | bytes 1540
  18.2 2.7 %collective-permute-start = (bf16[80,48,128]{2,1,0:T(8,128)(2,1)S(1)}, bf16[80,48,128]{2,1,0:T(8,128)(2,1)S(1)}, u32[]{:S(2)}, u32[]{:S(2)}) collective-permute-start(bf16[80,48,128]{2,1,0:T(8,128)(2,1)S(1)} %row_state.1.rest_0_), channel_id=1, source_target_pairs={{0,8},{8,0},{1,9},{9,1},{2,10},{10,2},{3,11},{11,3},{4,12},{12,4},... | collective-permute-start | bytes 2949128 | tf_op jit(solution)/shard_map/ppermute | solution.py:275
  20.9 0.9 copy-start.13
  21.9 10.1 %copy-start.3 = (bf16[128,512]{1,0:T(8,128)(2,1)S(1)}, bf16[128,512]{1,0:T(8,128)(2,1)}, u32[]{:S(2)}) copy-start(bf16[128,512]{1,0:T(8,128)(2,1)} %w.21) | copy-start | bytes 393220
  37.2 12.9 %collective-permute-start.1 = (bf16[1344,128]{1,0:T(8,128)(2,1)S(1)}, bf16[1344,128]{1,0:T(8,128)(2,1)S(1)}, u32[]{:S(2)}, u32[]{:S(2)}) collective-permute-start(bf16[1344,128]{1,0:T(8,128)(2,1)S(1)} %constant_dynamic-slice_fusion.11), channel_id=1, source_target_pairs={{0,1},{1,0},{2,3},{3,2},{4,5},{5,4},{6,7},{7,6},{8,9},{9,8},{10,11... | collective-permute-start | bytes 1032200 | tf_op jit(solution)/shard_map/ppermute | solution.py:199
  50.1 6.8 %collective-permute-start.2 = (bf16[672,128]{1,0:T(8,128)(2,1)S(1)}, bf16[672,128]{1,0:T(8,128)(2,1)S(1)}, u32[]{:S(2)}, u32[]{:S(2)}) collective-permute-start(bf16[672,128]{1,0:T(8,128)(2,1)S(1)} %constant_dynamic-slice_fusion.10), channel_id=1, source_target_pairs={{0,2},{1,3},{2,0},{3,1},{4,6},{5,7},{6,4},{7,5},{8,10},{9,11},{10,... | collective-permute-start | bytes 516104 | tf_op jit(solution)/shard_map/ppermute | solution.py:199
  57.0 6.7 %collective-permute-start.3 = (bf16[336,128]{1,0:T(8,128)(2,1)S(1)}, bf16[336,128]{1,0:T(8,128)(2,1)S(1)}, u32[]{:S(2)}, u32[]{:S(2)}) collective-permute-start(bf16[336,128]{1,0:T(8,128)(2,1)S(1)} %constant_dynamic-slice_fusion.9), channel_id=1, source_target_pairs={{0,4},{1,5},{2,6},{3,7},{4,0},{5,1},{6,2},{7,3},{8,12},{9,13},{10,... | collective-permute-start | bytes 258056 | tf_op jit(solution)/shard_map/ppermute | solution.py:199
  59.7 16.9 %collective-permute-start.5 = (bf16[1344,128]{1,0:T(8,128)(2,1)S(1)}, bf16[1344,128]{1,0:T(8,128)(2,1)S(1)}, u32[]{:S(2)}, u32[]{:S(2)}) collective-permute-start(bf16[1344,128]{1,0:T(8,128)(2,1)S(1)} %constant_dynamic-slice_fusion.8), channel_id=1, source_target_pairs={{0,2},{1,3},{2,0},{3,1},{4,6},{5,7},{6,4},{7,5},{8,10},{9,11},{10,... | collective-permute-start | bytes 1032200 | tf_op jit(solution)/shard_map/ppermute | solution.py:199
  63.8 12.3 %collective-permute-start.4 = (bf16[336,128]{1,0:T(8,128)(2,1)S(1)}, bf16[336,128]{1,0:T(8,128)(2,1)S(1)}, u32[]{:S(2)}, u32[]{:S(2)}) collective-permute-start(bf16[336,128]{1,0:T(8,128)(2,1)S(1)} %add_convert_fusion.11), channel_id=1, source_target_pairs={{0,4},{1,5},{2,6},{3,7},{4,0},{5,1},{6,2},{7,3},{8,12},{9,13},{10,... | collective-permute-start | bytes 258056 | tf_op jit(solution)/shard_map/ppermute | solution.py:205
  76.1 9.7 %collective-permute-start.7 = (bf16[672,128]{1,0:T(8,128)(2,1)S(1)}, bf16[672,128]{1,0:T(8,128)(2,1)S(1)}, u32[]{:S(2)}, u32[]{:S(2)}) collective-permute-start(bf16[672,128]{1,0:T(8,128)(2,1)S(1)} %maximum_select_fusion.4), channel_id=1, source_target_pairs={{0,2},{1,3},{2,0},{3,1},{4,6},{5,7},{6,4},{7,5},{8,10},{9,11},{10,... | collective-permute-start | bytes 516104 | tf_op jit(solution)/shard_map/ppermute | solution.py:205
  76.7 8.7 %collective-permute-start.6 = (bf16[672,128]{1,0:T(8,128)(2,1)S(1)}, bf16[672,128]{1,0:T(8,128)(2,1)S(1)}, u32[]{:S(2)}, u32[]{:S(2)}) collective-permute-start(bf16[672,128]{1,0:T(8,128)(2,1)S(1)} %constant_dynamic-slice_fusion.7), channel_id=1, source_target_pairs={{0,4},{1,5},{2,6},{3,7},{4,0},{5,1},{6,2},{7,3},{8,12},{9,13},{10,... | collective-permute-start | bytes 516104 | tf_op jit(solution)/shard_map/ppermute | solution.py:199
  82.8 25.7 %collective-permute-start.9 = (bf16[1344,128]{1,0:T(8,128)(2,1)S(1)}, bf16[1344,128]{1,0:T(8,128)(2,1)S(1)}, u32[]{:S(2)}, u32[]{:S(2)}) collective-permute-start(bf16[1344,128]{1,0:T(8,128)(2,1)S(1)} %constant_dynamic-slice_fusion.5), channel_id=1, source_target_pairs={{0,1},{1,0},{2,3},{3,2},{4,5},{5,4},{6,7},{7,6},{8,9},{9,8},{10,11... | collective-permute-start | bytes 1032200 | tf_op jit(solution)/shard_map/ppermute | solution.py:199
  85.6 10.1 %collective-permute-start.8 = (bf16[336,128]{1,0:T(8,128)(2,1)S(1)}, bf16[336,128]{1,0:T(8,128)(2,1)S(1)}, u32[]{:S(2)}, u32[]{:S(2)}) collective-permute-start(bf16[336,128]{1,0:T(8,128)(2,1)S(1)} %constant_dynamic-slice_fusion.6), channel_id=1, source_target_pairs={{0,1},{1,0},{2,3},{3,2},{4,5},{5,4},{6,7},{7,6},{8,9},{9,8},{10,11... | collective-permute-start | bytes 258056 | tf_op jit(solution)/shard_map/ppermute | solution.py:199
  85.9 35.3 %collective-permute-start.24 = (bf16[1344,128]{1,0:T(8,128)(2,1)S(1)}, bf16[1344,128]{1,0:T(8,128)(2,1)S(1)}, u32[]{:S(2)}, u32[]{:S(2)}) collective-permute-start(bf16[1344,128]{1,0:T(8,128)(2,1)S(1)} %maximum_select_fusion), channel_id=1, source_target_pairs={{0,1},{1,0},{2,3},{3,2},{4,5},{5,4},{6,7},{7,6},{8,9},{9,8},{10,11... | collective-permute-start | bytes 1032200 | tf_op jit(solution)/shard_map/ppermute | solution.py:205
  95.7 10.5 %collective-permute-start.21 = (bf16[336,128]{1,0:T(8,128)(2,1)S(1)}, bf16[336,128]{1,0:T(8,128)(2,1)S(1)}, u32[]{:S(2)}, u32[]{:S(2)}) collective-permute-start(bf16[336,128]{1,0:T(8,128)(2,1)S(1)} %add_convert_fusion.10), channel_id=1, source_target_pairs={{0,1},{1,0},{2,3},{3,2},{4,5},{5,4},{6,7},{7,6},{8,9},{9,8},{10,11... | collective-permute-start | bytes 258056 | tf_op jit(solution)/shard_map/ppermute | solution.py:205
  106.2 13.4 %collective-permute-start.22 = (bf16[672,128]{1,0:T(8,128)(2,1)S(1)}, bf16[672,128]{1,0:T(8,128)(2,1)S(1)}, u32[]{:S(2)}, u32[]{:S(2)}) collective-permute-start(bf16[672,128]{1,0:T(8,128)(2,1)S(1)} %maximum_select_fusion.7), channel_id=1, source_target_pairs={{0,4},{1,5},{2,6},{3,7},{4,0},{5,1},{6,2},{7,3},{8,12},{9,13},{10,... | collective-permute-start | bytes 516104 | tf_op jit(solution)/shard_map/ppermute | solution.py:205
  108.6 9.0 %collective-permute-start.16 = (bf16[672,128]{1,0:T(8,128)(2,1)S(1)}, bf16[672,128]{1,0:T(8,128)(2,1)S(1)}, u32[]{:S(2)}, u32[]{:S(2)}) collective-permute-start(bf16[672,128]{1,0:T(8,128)(2,1)S(1)} %constant_dynamic-slice_fusion.1), channel_id=1, source_target_pairs={{0,2},{1,3},{2,0},{3,1},{4,6},{5,7},{6,4},{7,5},{8,10},{9,11},{10,... | collective-permute-start | bytes 516104 | tf_op jit(solution)/shard_map/ppermute | solution.py:199
  115.2 6.2 %copy-start = (bf16[128,1024]{1,0:T(8,128)(2,1)S(1)}, bf16[128,1024]{1,0:T(8,128)(2,1)}, u32[]{:S(2)}) copy-start(bf16[128,1024]{1,0:T(8,128)(2,1)} %trans_in.11) | copy-start | bytes 786436
  115.2 6.2 %copy-start.4 = (bf16[512,128]{1,0:T(8,128)(2,1)S(1)}, bf16[512,128]{1,0:T(8,128)(2,1)}, u32[]{:S(2)}) copy-start(bf16[512,128]{1,0:T(8,128)(2,1)} %trans_out.11) | copy-start | bytes 393220
  115.2 6.2 %copy-start.6 = (bf16[128,128]{1,0:T(8,128)(2,1)S(1)}, bf16[128,128]{1,0:T(8,128)(2,1)}, u32[]{:S(2)}) copy-start(bf16[128,128]{1,0:T(8,128)(2,1)} %w_out.11) | copy-start | bytes 98308
  115.2 6.1 %copy-start.11 = (f32[128]{0:T(128)S(1)}, f32[128]{0:T(128)}, u32[]{:S(2)}) copy-start(f32[128]{0:T(128)} %param.20) | copy-start | bytes 1540
  115.2 6.1 %copy-start.12 = (f32[128]{0:T(128)S(1)}, f32[128]{0:T(128)}, u32[]{:S(2)}) copy-start(f32[128]{0:T(128)} %param.23) | copy-start | bytes 1540
  115.2 18.9 %collective-permute-start.10 = (bf16[1344,128]{1,0:T(8,128)(2,1)S(1)}, bf16[1344,128]{1,0:T(8,128)(2,1)S(1)}, u32[]{:S(2)}, u32[]{:S(2)}) collective-permute-start(bf16[1344,128]{1,0:T(8,128)(2,1)S(1)} %constant_dynamic-slice_fusion.4), channel_id=1, source_target_pairs={{0,2},{1,3},{2,0},{3,1},{4,6},{5,7},{6,4},{7,5},{8,10},{9,11},{10,... | collective-permute-start | bytes 1032200 | tf_op jit(solution)/shard_map/ppermute | solution.py:199
  117.6 14.9 %collective-permute-start.17 = (bf16[336,128]{1,0:T(8,128)(2,1)S(1)}, bf16[336,128]{1,0:T(8,128)(2,1)S(1)}, u32[]{:S(2)}, u32[]{:S(2)}) collective-permute-start(bf16[336,128]{1,0:T(8,128)(2,1)S(1)} %constant_dynamic-slice_fusion), channel_id=1, source_target_pairs={{0,4},{1,5},{2,6},{3,7},{4,0},{5,1},{6,2},{7,3},{8,12},{9,13},{10,... | collective-permute-start | bytes 258056 | tf_op jit(solution)/shard_map/ppermute | solution.py:199
  119.7 31.6 %collective-permute-start.23 = (bf16[1344,128]{1,0:T(8,128)(2,1)S(1)}, bf16[1344,128]{1,0:T(8,128)(2,1)S(1)}, u32[]{:S(2)}, u32[]{:S(2)}) collective-permute-start(bf16[1344,128]{1,0:T(8,128)(2,1)S(1)} %maximum_select_fusion.3), channel_id=1, source_target_pairs={{0,2},{1,3},{2,0},{3,1},{4,6},{5,7},{6,4},{7,5},{8,10},{9,11},{10,... | collective-permute-start | bytes 1032200 | tf_op jit(solution)/shard_map/ppermute | solution.py:205
  132.6 8.2 %collective-permute-start.18 = (bf16[336,128]{1,0:T(8,128)(2,1)S(1)}, bf16[336,128]{1,0:T(8,128)(2,1)S(1)}, u32[]{:S(2)}, u32[]{:S(2)}) collective-permute-start(bf16[336,128]{1,0:T(8,128)(2,1)S(1)} %add_convert_fusion.8), channel_id=1, source_target_pairs={{0,4},{1,5},{2,6},{3,7},{4,0},{5,1},{6,2},{7,3},{8,12},{9,13},{10,... | collective-permute-start | bytes 258056 | tf_op jit(solution)/shard_map/ppermute | solution.py:205
  134.3 14.7 %collective-permute-start.11 = (bf16[672,128]{1,0:T(8,128)(2,1)S(1)}, bf16[672,128]{1,0:T(8,128)(2,1)S(1)}, u32[]{:S(2)}, u32[]{:S(2)}) collective-permute-start(bf16[672,128]{1,0:T(8,128)(2,1)S(1)} %constant_dynamic-slice_fusion.3), channel_id=1, source_target_pairs={{0,4},{1,5},{2,6},{3,7},{4,0},{5,1},{6,2},{7,3},{8,12},{9,13},{10,... | collective-permute-start | bytes 516104 | tf_op jit(solution)/shard_map/ppermute | solution.py:199
  140.9 10.0 %collective-permute-start.19 = (bf16[672,128]{1,0:T(8,128)(2,1)S(1)}, bf16[672,128]{1,0:T(8,128)(2,1)S(1)}, u32[]{:S(2)}, u32[]{:S(2)}) collective-permute-start(bf16[672,128]{1,0:T(8,128)(2,1)S(1)} %maximum_select_fusion.6), channel_id=1, source_target_pairs={{0,2},{1,3},{2,0},{3,1},{4,6},{5,7},{6,4},{7,5},{8,10},{9,11},{10,... | collective-permute-start | bytes 516104 | tf_op jit(solution)/shard_map/ppermute | solution.py:205
  149.1 4.6 %collective-permute-start.12 = (bf16[336,128]{1,0:T(8,128)(2,1)S(1)}, bf16[336,128]{1,0:T(8,128)(2,1)S(1)}, u32[]{:S(2)}, u32[]{:S(2)}) collective-permute-start(bf16[336,128]{1,0:T(8,128)(2,1)S(1)} %constant_dynamic-slice_fusion.2), channel_id=1, source_target_pairs={{0,1},{1,0},{2,3},{3,2},{4,5},{5,4},{6,7},{7,6},{8,9},{9,8},{10,11... | collective-permute-start | bytes 258056 | tf_op jit(solution)/shard_map/ppermute | solution.py:199
  151.0 26.3 %collective-permute-start.20 = (bf16[1344,128]{1,0:T(8,128)(2,1)S(1)}, bf16[1344,128]{1,0:T(8,128)(2,1)S(1)}, u32[]{:S(2)}, u32[]{:S(2)}) collective-permute-start(bf16[1344,128]{1,0:T(8,128)(2,1)S(1)} %maximum_select_fusion.2), channel_id=1, source_target_pairs={{0,1},{1,0},{2,3},{3,2},{4,5},{5,4},{6,7},{7,6},{8,9},{9,8},{10,11... | collective-permute-start | bytes 1032200 | tf_op jit(solution)/shard_map/ppermute | solution.py:205
  153.7 12.9 %collective-permute-start.13 = (bf16[336,128]{1,0:T(8,128)(2,1)S(1)}, bf16[336,128]{1,0:T(8,128)(2,1)S(1)}, u32[]{:S(2)}, u32[]{:S(2)}) collective-permute-start(bf16[336,128]{1,0:T(8,128)(2,1)S(1)} %add_convert_fusion.9), channel_id=1, source_target_pairs={{0,1},{1,0},{2,3},{3,2},{4,5},{5,4},{6,7},{7,6},{8,9},{9,8},{10,11... | collective-permute-start | bytes 258056 | tf_op jit(solution)/shard_map/ppermute | solution.py:205
  166.6 8.4 %collective-permute-start.14 = (bf16[672,128]{1,0:T(8,128)(2,1)S(1)}, bf16[672,128]{1,0:T(8,128)(2,1)S(1)}, u32[]{:S(2)}, u32[]{:S(2)}) collective-permute-start(bf16[672,128]{1,0:T(8,128)(2,1)S(1)} %maximum_select_fusion.5), channel_id=1, source_target_pairs={{0,4},{1,5},{2,6},{3,7},{4,0},{5,1},{6,2},{7,3},{8,12},{9,13},{10,... | collective-permute-start | bytes 516104 | tf_op jit(solution)/shard_map/ppermute | solution.py:205
  175.2 19.6 %collective-permute-start.15 = (bf16[1344,128]{1,0:T(8,128)(2,1)S(1)}, bf16[1344,128]{1,0:T(8,128)(2,1)S(1)}, u32[]{:S(2)}, u32[]{:S(2)}) collective-permute-start(bf16[1344,128]{1,0:T(8,128)(2,1)S(1)} %maximum_select_fusion.1), channel_id=1, source_target_pairs={{0,2},{1,3},{2,0},{3,1},{4,6},{5,7},{6,4},{7,5},{8,10},{9,11},{10,... | collective-permute-start | bytes 1032200 | tf_op jit(solution)/shard_map/ppermute | solution.py:205
where the time goes:
time: 213 us; the launch traced here: 212 us
  Pallas kernels  149 us (70%)
  starting transfers between devices  32.7 us (15%)
  waiting for transfers between devices  23.9 us (11%)
  local copies, waits for them, and re-layouts  3.19 us (1%)
  other arithmetic  2.68 us (1%)
    pallas_call x6, Pallas kernels, shards(): pl.pallas_call(end_kernel, grid=(piece,), in_specs=[pl.BlockSpec((rows, t...  73.4 us
    pallas_call x4, Pallas kernels, shards(): pl.pallas_call(functools.partial(start_kernel, row_size), grid=(rows // g...  39.7 us
    pallas_call x4, Pallas kernels, shards(): pl.pallas_call(functools.partial(column_state_kernel, chunk * part), grid...  20.6 us
    ppermute x12, starting transfers between devices, exchange_sum(): got = lax.ppermute(sent, 'col', pairs)  17.2 us
    ppermute x12, waiting for transfers between devices, exchange_sum(): got = lax.ppermute(sent, 'col', pairs)  16.7 us
    pallas_call x1, Pallas kernels, shards(): pl.pallas_call(row_state_kernel, grid=(rows // group,), in_specs=[smem, p...  15 us
    ppermute x12, starting transfers between devices, exchange_sum(): got = lax.ppermute(values, 'col', pairs)  14.9 us
    ppermute x12, waiting for transfers between devices, exchange_sum(): got = lax.ppermute(values, 'col', pairs)  5.05 us
  transfers between devices with their start and end apart: 25, of which 7 were waited for; matrix products, arithmetic and copies ran while one was open for 1% of the time, Pallas kernels for 48%

commit v1 on v0

--- a/solution.py
+++ b/solution.py
@@ -79,7 +79,7 @@
     attended = numer * pl.reciprocal(jnp.maximum(denom, 1.0))
     square = matmul((attended * attended).astype(BF16), mean_matrix(numer.shape[-1]))
     scale = lax.rsqrt(square + EPSILON)
-    return (attended * scale * head_gain * sigmoid(gate)).astype(BF16)
+    return (attended * scale * head_gain * sigmoid(gate.astype(BF16)).astype(F32)).astype(BF16)
 
 
 def row_state_kernel(row_valid, pair, col_mask, gain, w, out):
@@ -88,8 +88,7 @@
     base = pl.program_id(0) * count
     normed = layer_norm([pair[...].reshape(count * cols, width)], gain[...])
     project = matmul(normed, w[:, width : 3 * width])
-    keys = feature(project[:, :width]).reshape(count, cols, width) * col_mask[...][None]
-    keys = keys.astype(BF16)
+    keys = feature(project[:, :width].astype(BF16)).reshape(count, cols, width) * col_mask[...].astype(BF16)[None]
     values = project[:, width:].reshape(count, cols, width).astype(BF16)
     for i in range(count):
         valid = row_valid[base + i]
@@ -108,7 +107,7 @@
     ones = same.astype(F32).astype(BF16)
     field = pair[...].reshape(count * cols, width)
     project = matmul(layer_norm([field], gain[...]), query_gate(w[...]))
-    queries = feature(project[:, :width]).reshape(count, cols, width).astype(BF16)
+    queries = feature(project[:, :width].astype(BF16)).reshape(count, cols, width).astype(BF16)
     numer, weighted = [], []
     for i in range(count):
         state = sum(s[i, 0:depth, :].astype(F32) for s in states)
@@ -137,8 +136,7 @@
     depth = width // HEADS
     base = first + pl.program_id(0) * count
     project = matmul(columns_first(normed, scratch), w[:, width : 3 * width])
-    keys = feature(project[:, :width]).reshape(count, rows, width) * row_mask[...][None]
-    keys = keys.astype(BF16)
+    keys = feature(project[:, :width].astype(BF16)).reshape(count, rows, width) * row_mask[...].astype(BF16)[None]
     values = project[:, width:].reshape(count, rows, width).astype(BF16)
     totals = []
     for j in range(count):
@@ -160,7 +158,7 @@
     same = same_head(width)
     ones = same.astype(F32).astype(BF16)
     project = matmul(columns_first(normed, scratch), query_gate(w[...]))
-    queries = feature(project[:, :width]).reshape(count, rows, width).astype(BF16)
+    queries = feature(project[:, :width].astype(BF16)).reshape(count, rows, width).astype(BF16)
     totals = state[0, count * depth : count * (depth + 1), :].astype(F32)
     numer, weighted = [], []
     for j in range(count):
@@ -187,22 +185,27 @@
     update_trans[...] = moved.astype(BF16).reshape(rows, count, width)
 
 
-def exchange_sum(values, size, bits, done):
+def exchange_sum(values, size, bits, done, last):
+    def after(got):
+        return lax.optimization_barrier((got, last[-1]))[0] if last else got
+
     me = lax.axis_index("col")
     for bit in bits:
-        yield values
         half = values.shape[0] // 2
         mine = (me >> bit) & 1
         pairs = [(d, d ^ (1 << bit)) for d in range(size)]
         sent = lax.dynamic_slice_in_dim(values, (1 - mine) * half, half)
         kept = lax.dynamic_slice_in_dim(values, mine * half, half)
         got = lax.ppermute(sent, "col", pairs)
+        yield values
+        got = after(got)
         values = (kept.astype(F32) + got.astype(F32)).astype(BF16)
     for bit in reversed(bits):
-        yield values
         mine = (me >> bit) & 1
         pairs = [(d, d ^ (1 << bit)) for d in range(size)]
         got = lax.ppermute(values, "col", pairs)
+        yield values
+        got = after(got)
         values = jnp.where(
             mine == 1,
             jnp.concatenate([got, values], axis=0),
@@ -284,7 +287,7 @@
     pad = -(tiles * block) % (16 * size)
     bits = list(range(size.bit_length() - 1))
     full = jax.ShapeDtypeStruct(pair.shape, BF16)
-    flying = []
+    flying, last = [], []
 
     def advance(small):
         for steps in list(flying):
@@ -331,6 +334,7 @@
             *extra,
         )
         normed_parts.append(normed)
+        last[:] = [normed]
         state = pl.pallas_call(
             functools.partial(column_state_kernel, chunk * part),
             grid=(tiles,),
@@ -348,12 +352,14 @@
             name="column_state",
         )(col_valid, normed, advance(row_mask), end_in)
         order = bits if chunk % 2 == 0 else bits[1:] + bits[:1]
+        last[:] = [state]
         state = jnp.pad(state.reshape(tiles * block, width), ((0, pad), (0, 0)))
         column_states.append([])
-        flying.append(exchange_sum(state, size, order, column_states[-1]))
+        flying.append(exchange_sum(state, size, order, column_states[-1], last))
 
     outs = []
     for chunk in range(chunks):
+        last[:] = []
         done = 0
         pieces = [(tiles + 1) // 2, tiles // 2] if 2 * chunk < chunks else [tiles]
         for piece in pieces:

time: 213 us -> 210 us (0.986)
  transfers between devices with their start and end apart: 25 -> 25, of which waited for: 7 -> 7; matrix products, arithmetic and copies ran while one was open for 1% -> 1% of each run, Pallas kernels for 48% -> 46%
where the time goes in v1:
time: 210 us; the launch traced here: 209 us
  Pallas kernels  149 us (71%)
  starting transfers between devices  31.6 us (15%)
  waiting for transfers between devices  21.8 us (10%)
  local copies, waits for them, and re-layouts  3.17 us (2%)
  other arithmetic  2.68 us (1%)
    pallas_call x6, Pallas kernels, shards(): pl.pallas_call(end_kernel, grid=(piece,), in_specs=[pl.BlockSpec((rows, t...  73.5 us
    pallas_call x4, Pallas kernels, shards(): pl.pallas_call(functools.partial(start_kernel, row_size), grid=(rows // g...  40.3 us
    pallas_call x4, Pallas kernels, shards(): pl.pallas_call(functools.partial(column_state_kernel, chunk * part), grid...  20.3 us
    ppermute x12, starting transfers between devices, exchange_sum(): got = lax.ppermute(sent, 'col', pairs)  17.9 us
    pallas_call x1, Pallas kernels, shards(): pl.pallas_call(row_state_kernel, grid=(rows // group,), in_specs=[smem, p...  15 us
    ppermute x12, waiting for transfers between devices, exchange_sum(): got = lax.ppermute(sent, 'col', pairs)  14.6 us
    ppermute x12, starting transfers between devices, exchange_sum(): got = lax.ppermute(values, 'col', pairs)  13.2 us
    ppermute x12, waiting for transfers between devices, exchange_sum(): got = lax.ppermute(values, 'col', pairs)  4.97 us
  transfers between devices with their start and end apart: 25, of which 7 were waited for; matrix products, arithmetic and copies ran while one was open for 1% of the time, Pallas kernels for 46%

profile of v1, /device:TPU:0, one launch (start us, length us, event | category | flops | bytes accessed | tf_op | source)
XLA Modules:
  0.0 209.5 jit_solution(11025004894775005703)
XLA Ops:
  0.6 0.7 convert_element_type.116
  1.6 0.9 copy-done.1
  2.5 0.7 copy-done.7
  3.2 15.0 %row_state.1.rest_0_ = bf16[80,48,128]{2,1,0:T(8,128)(2,1)S(1)} custom-call(f32[80]{0:T(128)S(1)} %dynamic_slice.78.row_valid, bf16[80,320,128]{2,1,0:T(8,128)(2,1)} %pair.21, f32[320,128]{1,0:T(8,128)S(1)} %broadcast_in_dim.4.col_mask, f32[1,128]{1,0:T(1,128)S(1)} %bitcast.27, bf16[128,512]{1,0:T(8,128)(2,1)S(1)} %copy-done.1), custom_call_target="tpu_custom_call" | custom-call | flops 20000000000 | bytes 1048576 | tf_op jit(solution)/shard_map/row_state/pallas_call | solution.py:261
  18.2 0.5 collective-permute-start
  18.7 2.2 %collective-permute-done.rest_1_ = bf16[80,48,128]{2,1,0:T(8,128)(2,1)S(1)} collective-permute-done((bf16[80,48,128]{2,1,0:T(8,128)(2,1)S(1)}, bf16[80,48,128]{2,1,0:T(8,128)(2,1)S(1)}, u32[]{:S(2)}, u32[]{:S(2)}) %collective-permute-start) | collective-permute-done | bytes 983072 | tf_op jit(solution)/shard_map/ppermute | solution.py:278
  20.9 0.9 copy-done.13
  21.9 10.1 %start_finish.4 = (bf16[80,320,128]{2,1,0:T(8,128)(2,1)}, bf16[80,80,128]{2,1,0:T(8,128)(2,1)}) custom-call(bf16[80,320,128]{2,1,0:T(8,128)(2,1)} %pair.21, bf16[80,48,128]{2,1,0:T(8,128)(2,1)S(1)} %row_state.1.rest_0_, bf16[80,48,128]{2,1,0:T(8,128)(2,1)} %copy-done.13, f32[1,128]{1,0:T(1,128)S(1)} %bitcast.28, f32[1,128]{1,0:T(1,128)S(1)} %bitcast.32, ...), custom_call_target="tpu_custom_call" | custom-call | flops 10000000000 | bytes 1048576 | tf_op jit(solution)/shard_map/start_finish/pallas_call | solution.py:307
  32.1 5.1 %column_state.4 = bf16[5,528,128]{2,1,0:T(8,128)(2,1)S(1)} custom-call(f32[320]{0:T(512)S(1)} %dynamic_slice.79.col_valid, bf16[80,80,128]{2,1,0:T(8,128)(2,1)} %get-tuple-element.56.normed, f32[80,128]{1,0:T(8,128)S(1)} %broadcast_in_dim.5.row_mask, bf16[128,512]{1,0:T(8,128)(2,1)S(1)} %copy-done.3), custom_call_target="tpu_custom_call" | custom-call | flops 6000000000 | bytes 1048576 | tf_op jit(solution)/shard_map/column_state/pallas_call | solution.py:338
  37.2 3.0 %collective-permute-start.1 = (bf16[1344,128]{1,0:T(8,128)(2,1)S(1)}, bf16[1344,128]{1,0:T(8,128)(2,1)S(1)}, u32[]{:S(2)}, u32[]{:S(2)}) collective-permute-start(bf16[1344,128]{1,0:T(8,128)(2,1)S(1)} %constant_dynamic-slice_fusion.11), channel_id=1, source_target_pairs={{0,1},{1,0},{2,3},{3,2},{4,5},{5,4},{6,7},{7,6},{8,9},{9,8},{10,11... | collective-permute-start | bytes 1032200 | tf_op jit(solution)/shard_map/ppermute | solution.py:199
  40.2 10.0 %start_finish.5 = (bf16[80,320,128]{2,1,0:T(8,128)(2,1)}, bf16[80,80,128]{2,1,0:T(8,128)(2,1)}) custom-call(bf16[80,320,128]{2,1,0:T(8,128)(2,1)} %pair.21, bf16[80,48,128]{2,1,0:T(8,128)(2,1)S(1)} %row_state.1.rest_0_, bf16[80,48,128]{2,1,0:T(8,128)(2,1)} %copy-done.13, f32[1,128]{1,0:T(1,128)S(1)} %bitcast.29, ...), custom_call_target="tpu_custom_call", output_to_operand_aliasing={{0}: (8, {})} | custom-call | flops 10000000000 | bytes 1048576 | tf_op jit(solution)/shard_map/start_finish/pallas_call | solution.py:307
  50.3 5.1 %column_state.5 = bf16[5,528,128]{2,1,0:T(8,128)(2,1)S(1)} custom-call(f32[320]{0:T(512)S(1)} %dynamic_slice.79.col_valid, bf16[80,80,128]{2,1,0:T(8,128)(2,1)} %get-tuple-element.59.normed, f32[80,128]{1,0:T(8,128)S(1)} %broadcast_in_dim.5.row_mask, bf16[128,512]{1,0:T(8,128)(2,1)S(1)} %copy-done.3), custom_call_target="tpu_custom_call" | custom-call | flops 6000000000 | bytes 1048576 | tf_op jit(solution)/shard_map/column_state/pallas_call | solution.py:338
  55.5 1.6 collective-permute-start.2
  57.1 0.5 collective-permute-start.5
  57.7 5.1 %collective-permute-done.2 = bf16[672,128]{1,0:T(8,128)(2,1)S(1)} collective-permute-done((bf16[672,128]{1,0:T(8,128)(2,1)S(1)}, bf16[672,128]{1,0:T(8,128)(2,1)S(1)}, u32[]{:S(2)}, u32[]{:S(2)}) %collective-permute-start.2) | collective-permute-done | bytes 172064 | tf_op jit(solution)/shard_map/ppermute | solution.py:199
  62.9 2.6 %collective-permute-start.3 = (bf16[336,128]{1,0:T(8,128)(2,1)S(1)}, bf16[336,128]{1,0:T(8,128)(2,1)S(1)}, u32[]{:S(2)}, u32[]{:S(2)}) collective-permute-start(bf16[336,128]{1,0:T(8,128)(2,1)S(1)} %constant_dynamic-slice_fusion.9), channel_id=1, source_target_pairs={{0,4},{1,5},{2,6},{3,7},{4,0},{5,1},{6,2},{7,3},{8,12},{9,13},{10,... | collective-permute-start | bytes 258056 | tf_op jit(solution)/shard_map/ppermute | solution.py:199
  65.5 10.1 %start_finish.6 = (bf16[80,320,128]{2,1,0:T(8,128)(2,1)}, bf16[80,80,128]{2,1,0:T(8,128)(2,1)}) custom-call(bf16[80,320,128]{2,1,0:T(8,128)(2,1)} %pair.21, bf16[80,48,128]{2,1,0:T(8,128)(2,1)S(1)} %row_state.1.rest_0_, bf16[80,48,128]{2,1,0:T(8,128)(2,1)} %copy-done.13, f32[1,128]{1,0:T(1,128)S(1)} %bitcast.30, ...), custom_call_target="tpu_custom_call", output_to_operand_aliasing={{0}: (8, {})} | custom-call | flops 10000000000 | bytes 1048576 | tf_op jit(solution)/shard_map/start_finish/pallas_call | solution.py:307
  75.6 0.4 collective-permute-start.4
  76.1 5.1 %column_state.6 = bf16[5,528,128]{2,1,0:T(8,128)(2,1)S(1)} custom-call(f32[320]{0:T(512)S(1)} %dynamic_slice.79.col_valid, bf16[80,80,128]{2,1,0:T(8,128)(2,1)} %get-tuple-element.66.normed, f32[80,128]{1,0:T(8,128)S(1)} %broadcast_in_dim.5.row_mask, bf16[128,512]{1,0:T(8,128)(2,1)S(1)} %copy-done.3), custom_call_target="tpu_custom_call" | custom-call | flops 6000000000 | bytes 1048576 | tf_op jit(solution)/shard_map/column_state/pallas_call | solution.py:338
  81.3 1.6 collective-permute-start.7
  82.9 2.7 %collective-permute-start.6 = (bf16[672,128]{1,0:T(8,128)(2,1)S(1)}, bf16[672,128]{1,0:T(8,128)(2,1)S(1)}, u32[]{:S(2)}, u32[]{:S(2)}) collective-permute-start(bf16[672,128]{1,0:T(8,128)(2,1)S(1)} %constant_dynamic-slice_fusion.7), channel_id=1, source_target_pairs={{0,4},{1,5},{2,6},{3,7},{4,0},{5,1},{6,2},{7,3},{8,12},{9,13},{10,... | collective-permute-start | bytes 516104 | tf_op jit(solution)/shard_map/ppermute | solution.py:199
  85.6 0.6 collective-permute-start.9
  86.2 4.9 %collective-permute-done.6 = bf16[672,128]{1,0:T(8,128)(2,1)S(1)} collective-permute-done((bf16[672,128]{1,0:T(8,128)(2,1)S(1)}, bf16[672,128]{1,0:T(8,128)(2,1)S(1)}, u32[]{:S(2)}, u32[]{:S(2)}) %collective-permute-start.6) | collective-permute-done | bytes 172064 | tf_op jit(solution)/shard_map/ppermute | solution.py:199
  91.2 0.6 collective-permute-start.8
  91.8 10.1 %start_finish.7 = (bf16[80,320,128]{2,1,0:T(8,128)(2,1)}, bf16[80,80,128]{2,1,0:T(8,128)(2,1)}) custom-call(bf16[80,320,128]{2,1,0:T(8,128)(2,1)} %pair.21, bf16[80,48,128]{2,1,0:T(8,128)(2,1)S(1)} %row_state.1.rest_0_, bf16[80,48,128]{2,1,0:T(8,128)(2,1)} %copy-done.13, f32[1,128]{1,0:T(1,128)S(1)} %bitcast.31, ...), custom_call_target="tpu_custom_call", output_to_operand_aliasing={{0}: (8, {})} | custom-call | flops 10000000000 | bytes 1048576 | tf_op jit(solution)/shard_map/start_finish/pallas_call | solution.py:307
  101.9 1.6 collective-permute-start.21
  103.6 0.6 collective-permute-start.24
  104.2 2.3 %collective-permute-done.21 = bf16[336,128]{1,0:T(8,128)(2,1)S(1)} collective-permute-done((bf16[336,128]{1,0:T(8,128)(2,1)S(1)}, bf16[336,128]{1,0:T(8,128)(2,1)S(1)}, u32[]{:S(2)}, u32[]{:S(2)}) %collective-permute-start.21) | collective-permute-done | bytes 86048 | tf_op jit(solution)/shard_map/ppermute | solution.py:206
  106.5 1.2 collective-permute-start.22
  107.8 2.0 collective-permute-start.16
  109.8 5.1 %column_state.7 = bf16[5,528,128]{2,1,0:T(8,128)(2,1)S(1)} custom-call(f32[320]{0:T(512)S(1)} %dynamic_slice.79.col_valid, bf16[80,80,128]{2,1,0:T(8,128)(2,1)} %get-tuple-element.78.normed, f32[80,128]{1,0:T(8,128)S(1)} %broadcast_in_dim.5.row_mask, bf16[128,512]{1,0:T(8,128)(2,1)S(1)} %copy-done.3), custom_call_target="tpu_custom_call" | custom-call | flops 6000000000 | bytes 1048576 | tf_op jit(solution)/shard_map/column_state/pallas_call | solution.py:338
  115.0 0.3 collective-permute-start.10
  115.3 2.4 %collective-permute-done.16 = bf16[672,128]{1,0:T(8,128)(2,1)S(1)} collective-permute-done((bf16[672,128]{1,0:T(8,128)(2,1)S(1)}, bf16[672,128]{1,0:T(8,128)(2,1)S(1)}, u32[]{:S(2)}, u32[]{:S(2)}) %collective-permute-start.16) | collective-permute-done | bytes 172064 | tf_op jit(solution)/shard_map/ppermute | solution.py:199
  118.1 2.1 collective-permute-start.23
  120.5 11.2 %end_finish.6 = (bf16[80,320,128]{2,1,0:T(8,128)(2,1)}, bf16[80,320,128]{2,1,0:T(8,128)(2,1)}) custom-call(bf16[80,80,128]{2,1,0:T(8,128)(2,1)} %get-tuple-element.56.normed, bf16[80,320,128]{2,1,0:T(8,128)(2,1)} %pair.21, bf16[80,320,128]{2,1,0:T(8,128)(2,1)} %get-tuple-element.53.update_start, bf16[5,528,128]{2,1,0:T(8,128)(2,1)S(1)} %bitcast.21, ...), custom_call_target="tpu_custom_call" | custom-call | flops 10000000000 | bytes 1048576 | tf_op jit(solution)/shard_map/end_finish/pallas_call | solution.py:375
  131.7 0.8 collective-permute-start.18
  132.7 2.3 %collective-permute-start.11 = (bf16[672,128]{1,0:T(8,128)(2,1)S(1)}, bf16[672,128]{1,0:T(8,128)(2,1)S(1)}, u32[]{:S(2)}, u32[]{:S(2)}) collective-permute-start(bf16[672,128]{1,0:T(8,128)(2,1)S(1)} %constant_dynamic-slice_fusion.3), channel_id=1, source_target_pairs={{0,4},{1,5},{2,6},{3,7},{4,0},{5,1},{6,2},{7,3},{8,12},{9,13},{10,... | collective-permute-start | bytes 516104 | tf_op jit(solution)/shard_map/ppermute | solution.py:199
  134.9 2.6 %collective-permute-done.18 = bf16[336,128]{1,0:T(8,128)(2,1)S(1)} collective-permute-done((bf16[336,128]{1,0:T(8,128)(2,1)S(1)}, bf16[336,128]{1,0:T(8,128)(2,1)S(1)}, u32[]{:S(2)}, u32[]{:S(2)}) %collective-permute-start.18) | collective-permute-done | bytes 86048 | tf_op jit(solution)/shard_map/ppermute | solution.py:206
  137.7 8.1 %end_finish.7 = (bf16[80,320,128]{2,1,0:T(8,128)(2,1)}, bf16[80,320,128]{2,1,0:T(8,128)(2,1)}) custom-call(bf16[80,80,128]{2,1,0:T(8,128)(2,1)} %get-tuple-element.56.normed, bf16[80,320,128]{2,1,0:T(8,128)(2,1)} %pair.21, bf16[80,320,128]{2,1,0:T(8,128)(2,1)} %get-tuple-element.53.update_start, ...), custom_call_target="tpu_custom_call", output_to_operand_aliasing={{0}: (10, {}), {1}: (11, {})} | custom-call | flops 10000000000 | bytes 1048576 | tf_op jit(solution)/shard_map/end_finish/pallas_call | solution.py:375
  145.9 1.6 collective-permute-start.12
  147.6 0.6 collective-permute-start.20
  148.3 2.1 %collective-permute-done.12 = bf16[336,128]{1,0:T(8,128)(2,1)S(1)} collective-permute-done((bf16[336,128]{1,0:T(8,128)(2,1)S(1)}, bf16[336,128]{1,0:T(8,128)(2,1)S(1)}, u32[]{:S(2)}, u32[]{:S(2)}) %collective-permute-start.12) | collective-permute-done | bytes 86048 | tf_op jit(solution)/shard_map/ppermute | solution.py:199
  150.5 1.6 collective-permute-start.13
  152.1 11.2 %end_finish.8 = (bf16[80,320,128]{2,1,0:T(8,128)(2,1)}, bf16[80,320,128]{2,1,0:T(8,128)(2,1)}) custom-call(bf16[80,80,128]{2,1,0:T(8,128)(2,1)} %get-tuple-element.59.normed, bf16[80,320,128]{2,1,0:T(8,128)(2,1)} %pair.21, bf16[80,320,128]{2,1,0:T(8,128)(2,1)} %get-tuple-element.53.update_start, ...), custom_call_target="tpu_custom_call", output_to_operand_aliasing={{0}: (10, {}), {1}: (11, {})} | custom-call | flops 10000000000 | bytes 1048576 | tf_op jit(solution)/shard_map/end_finish/pallas_call | solution.py:375
  163.3 2.6 %collective-permute-start.14 = (bf16[672,128]{1,0:T(8,128)(2,1)S(1)}, bf16[672,128]{1,0:T(8,128)(2,1)S(1)}, u32[]{:S(2)}, u32[]{:S(2)}) collective-permute-start(bf16[672,128]{1,0:T(8,128)(2,1)S(1)} %maximum_select_fusion.5), channel_id=1, source_target_pairs={{0,4},{1,5},{2,6},{3,7},{4,0},{5,1},{6,2},{7,3},{8,12},{9,13},{10,... | collective-permute-start | bytes 516104 | tf_op jit(solution)/shard_map/ppermute | solution.py:206
  165.9 8.1 %end_finish.9 = (bf16[80,320,128]{2,1,0:T(8,128)(2,1)}, bf16[80,320,128]{2,1,0:T(8,128)(2,1)}) custom-call(bf16[80,80,128]{2,1,0:T(8,128)(2,1)} %get-tuple-element.59.normed, bf16[80,320,128]{2,1,0:T(8,128)(2,1)} %pair.21, bf16[80,320,128]{2,1,0:T(8,128)(2,1)} %get-tuple-element.53.update_start, ...), custom_call_target="tpu_custom_call", output_to_operand_aliasing={{0}: (10, {}), {1}: (11, {})} | custom-call | flops 10000000000 | bytes 1048576 | tf_op jit(solution)/shard_map/end_finish/pallas_call | solution.py:375
  174.5 17.4 %end_finish.10 = (bf16[80,320,128]{2,1,0:T(8,128)(2,1)}, bf16[80,320,128]{2,1,0:T(8,128)(2,1)}) custom-call(bf16[80,80,128]{2,1,0:T(8,128)(2,1)} %get-tuple-element.66.normed, bf16[80,320,128]{2,1,0:T(8,128)(2,1)} %pair.21, bf16[80,320,128]{2,1,0:T(8,128)(2,1)} %get-tuple-element.53.update_start, ...), custom_call_target="tpu_custom_call", output_to_operand_aliasing={{0}: (10, {}), {1}: (11, {})} | custom-call | flops 10000000000 | bytes 1048576 | tf_op jit(solution)/shard_map/end_finish/pallas_call | solution.py:375
  192.1 17.4 %end_finish.11 = (bf16[80,320,128]{2,1,0:T(8,128)(2,1)}, bf16[80,320,128]{2,1,0:T(8,128)(2,1)}) custom-call(bf16[80,80,128]{2,1,0:T(8,128)(2,1)} %get-tuple-element.78.normed, bf16[80,320,128]{2,1,0:T(8,128)(2,1)} %pair.21, bf16[80,320,128]{2,1,0:T(8,128)(2,1)} %get-tuple-element.53.update_start, ...), custom_call_target="tpu_custom_call", output_to_operand_aliasing={{0}: (10, {}), {1}: (11, {})} | custom-call | flops 10000000000 | bytes 1048576 | tf_op jit(solution)/shard_map/end_finish/pallas_call | solution.py:375
  (86 shorter events, 3.1 us)
Async XLA Ops:
  1.6 0.9 copy-start.1
  2.5 0.7 copy-start.7
  3.2 18.7 %copy-start.2 = (bf16[128,512]{1,0:T(8,128)(2,1)S(1)}, bf16[128,512]{1,0:T(8,128)(2,1)}, u32[]{:S(2)}) copy-start(bf16[128,512]{1,0:T(8,128)(2,1)} %rest_4_.7) | copy-start | bytes 393220
  3.2 18.7 %copy-start.5 = (bf16[128,128]{1,0:T(8,128)(2,1)S(1)}, bf16[128,128]{1,0:T(8,128)(2,1)}, u32[]{:S(2)}) copy-start(bf16[128,128]{1,0:T(8,128)(2,1)} %rest_5_.7) | copy-start | bytes 98308
  3.2 18.7 %copy-start.8 = (f32[128]{0:T(128)S(1)}, f32[128]{0:T(128)}, u32[]{:S(2)}) copy-start(f32[128]{0:T(128)} %param.15) | copy-start | bytes 1540
  3.2 18.7 %copy-start.9 = (f32[128]{0:T(128)S(1)}, f32[128]{0:T(128)}, u32[]{:S(2)}) copy-start(f32[128]{0:T(128)} %param.16) | copy-start | bytes 1540
  3.2 18.7 %copy-start.10 = (f32[128]{0:T(128)S(1)}, f32[128]{0:T(128)}, u32[]{:S(2)}) copy-start(f32[128]{0:T(128)} %param.19) | copy-start | bytes 1540
  18.2 2.7 %collective-permute-start = (bf16[80,48,128]{2,1,0:T(8,128)(2,1)S(1)}, bf16[80,48,128]{2,1,0:T(8,128)(2,1)S(1)}, u32[]{:S(2)}, u32[]{:S(2)}) collective-permute-start(bf16[80,48,128]{2,1,0:T(8,128)(2,1)S(1)} %row_state.1.rest_0_), channel_id=1, source_target_pairs={{0,8},{8,0},{1,9},{9,1},{2,10},{10,2},{3,11},{11,3},{4,12},{12,4},... | collective-permute-start | bytes 2949128 | tf_op jit(solution)/shard_map/ppermute | solution.py:278
  20.9 0.9 copy-start.13
  21.9 10.2 %copy-start.3 = (bf16[128,512]{1,0:T(8,128)(2,1)S(1)}, bf16[128,512]{1,0:T(8,128)(2,1)}, u32[]{:S(2)}) copy-start(bf16[128,512]{1,0:T(8,128)(2,1)} %w.21) | copy-start | bytes 393220
  37.2 13.0 %collective-permute-start.1 = (bf16[1344,128]{1,0:T(8,128)(2,1)S(1)}, bf16[1344,128]{1,0:T(8,128)(2,1)S(1)}, u32[]{:S(2)}, u32[]{:S(2)}) collective-permute-start(bf16[1344,128]{1,0:T(8,128)(2,1)S(1)} %constant_dynamic-slice_fusion.11), channel_id=1, source_target_pairs={{0,1},{1,0},{2,3},{3,2},{4,5},{5,4},{6,7},{7,6},{8,9},{9,8},{10,11... | collective-permute-start | bytes 1032200 | tf_op jit(solution)/shard_map/ppermute | solution.py:199
  55.5 7.3 %collective-permute-start.2 = (bf16[672,128]{1,0:T(8,128)(2,1)S(1)}, bf16[672,128]{1,0:T(8,128)(2,1)S(1)}, u32[]{:S(2)}, u32[]{:S(2)}) collective-permute-start(bf16[672,128]{1,0:T(8,128)(2,1)S(1)} %constant_dynamic-slice_fusion.10), channel_id=1, source_target_pairs={{0,2},{1,3},{2,0},{3,1},{4,6},{5,7},{6,4},{7,5},{8,10},{9,11},{10,... | collective-permute-start | bytes 516104 | tf_op jit(solution)/shard_map/ppermute | solution.py:199
  57.1 18.9 %collective-permute-start.5 = (bf16[1344,128]{1,0:T(8,128)(2,1)S(1)}, bf16[1344,128]{1,0:T(8,128)(2,1)S(1)}, u32[]{:S(2)}, u32[]{:S(2)}) collective-permute-start(bf16[1344,128]{1,0:T(8,128)(2,1)S(1)} %constant_dynamic-slice_fusion.8), channel_id=1, source_target_pairs={{0,2},{1,3},{2,0},{3,1},{4,6},{5,7},{6,4},{7,5},{8,10},{9,11},{10,... | collective-permute-start | bytes 1032200 | tf_op jit(solution)/shard_map/ppermute | solution.py:199
  62.9 12.7 %collective-permute-start.3 = (bf16[336,128]{1,0:T(8,128)(2,1)S(1)}, bf16[336,128]{1,0:T(8,128)(2,1)S(1)}, u32[]{:S(2)}, u32[]{:S(2)}) collective-permute-start(bf16[336,128]{1,0:T(8,128)(2,1)S(1)} %constant_dynamic-slice_fusion.9), channel_id=1, source_target_pairs={{0,4},{1,5},{2,6},{3,7},{4,0},{5,1},{6,2},{7,3},{8,12},{9,13},{10,... | collective-permute-start | bytes 258056 | tf_op jit(solution)/shard_map/ppermute | solution.py:199
  75.6 5.6 %collective-permute-start.4 = (bf16[336,128]{1,0:T(8,128)(2,1)S(1)}, bf16[336,128]{1,0:T(8,128)(2,1)S(1)}, u32[]{:S(2)}, u32[]{:S(2)}) collective-permute-start(bf16[336,128]{1,0:T(8,128)(2,1)S(1)} %add_convert_fusion.11), channel_id=1, source_target_pairs={{0,4},{1,5},{2,6},{3,7},{4,0},{5,1},{6,2},{7,3},{8,12},{9,13},{10,... | collective-permute-start | bytes 258056 | tf_op jit(solution)/shard_map/ppermute | solution.py:206
  81.3 20.6 %collective-permute-start.7 = (bf16[672,128]{1,0:T(8,128)(2,1)S(1)}, bf16[672,128]{1,0:T(8,128)(2,1)S(1)}, u32[]{:S(2)}, u32[]{:S(2)}) collective-permute-start(bf16[672,128]{1,0:T(8,128)(2,1)S(1)} %maximum_select_fusion.4), channel_id=1, source_target_pairs={{0,2},{1,3},{2,0},{3,1},{4,6},{5,7},{6,4},{7,5},{8,10},{9,11},{10,... | collective-permute-start | bytes 516104 | tf_op jit(solution)/shard_map/ppermute | solution.py:206
  82.9 8.2 %collective-permute-start.6 = (bf16[672,128]{1,0:T(8,128)(2,1)S(1)}, bf16[672,128]{1,0:T(8,128)(2,1)S(1)}, u32[]{:S(2)}, u32[]{:S(2)}) collective-permute-start(bf16[672,128]{1,0:T(8,128)(2,1)S(1)} %constant_dynamic-slice_fusion.7), channel_id=1, source_target_pairs={{0,4},{1,5},{2,6},{3,7},{4,0},{5,1},{6,2},{7,3},{8,12},{9,13},{10,... | collective-permute-start | bytes 516104 | tf_op jit(solution)/shard_map/ppermute | solution.py:199
  85.6 22.1 %collective-permute-start.9 = (bf16[1344,128]{1,0:T(8,128)(2,1)S(1)}, bf16[1344,128]{1,0:T(8,128)(2,1)S(1)}, u32[]{:S(2)}, u32[]{:S(2)}) collective-permute-start(bf16[1344,128]{1,0:T(8,128)(2,1)S(1)} %constant_dynamic-slice_fusion.5), channel_id=1, source_target_pairs={{0,1},{1,0},{2,3},{3,2},{4,5},{5,4},{6,7},{7,6},{8,9},{9,8},{10,11... | collective-permute-start | bytes 1032200 | tf_op jit(solution)/shard_map/ppermute | solution.py:199
  91.2 10.6 %collective-permute-start.8 = (bf16[336,128]{1,0:T(8,128)(2,1)S(1)}, bf16[336,128]{1,0:T(8,128)(2,1)S(1)}, u32[]{:S(2)}, u32[]{:S(2)}) collective-permute-start(bf16[336,128]{1,0:T(8,128)(2,1)S(1)} %constant_dynamic-slice_fusion.6), channel_id=1, source_target_pairs={{0,1},{1,0},{2,3},{3,2},{4,5},{5,4},{6,7},{7,6},{8,9},{9,8},{10,11... | collective-permute-start | bytes 258056 | tf_op jit(solution)/shard_map/ppermute | solution.py:199
  101.9 4.6 %collective-permute-start.21 = (bf16[336,128]{1,0:T(8,128)(2,1)S(1)}, bf16[336,128]{1,0:T(8,128)(2,1)S(1)}, u32[]{:S(2)}, u32[]{:S(2)}) collective-permute-start(bf16[336,128]{1,0:T(8,128)(2,1)S(1)} %add_convert_fusion.10), channel_id=1, source_target_pairs={{0,1},{1,0},{2,3},{3,2},{4,5},{5,4},{6,7},{7,6},{8,9},{9,8},{10,11... | collective-permute-start | bytes 258056 | tf_op jit(solution)/shard_map/ppermute | solution.py:206
  103.6 16.7 %collective-permute-start.24 = (bf16[1344,128]{1,0:T(8,128)(2,1)S(1)}, bf16[1344,128]{1,0:T(8,128)(2,1)S(1)}, u32[]{:S(2)}, u32[]{:S(2)}) collective-permute-start(bf16[1344,128]{1,0:T(8,128)(2,1)S(1)} %maximum_select_fusion), channel_id=1, source_target_pairs={{0,1},{1,0},{2,3},{3,2},{4,5},{5,4},{6,7},{7,6},{8,9},{9,8},{10,11... | collective-permute-start | bytes 1032200 | tf_op jit(solution)/shard_map/ppermute | solution.py:206
  106.5 11.5 %collective-permute-start.22 = (bf16[672,128]{1,0:T(8,128)(2,1)S(1)}, bf16[672,128]{1,0:T(8,128)(2,1)S(1)}, u32[]{:S(2)}, u32[]{:S(2)}) collective-permute-start(bf16[672,128]{1,0:T(8,128)(2,1)S(1)} %maximum_select_fusion.7), channel_id=1, source_target_pairs={{0,4},{1,5},{2,6},{3,7},{4,0},{5,1},{6,2},{7,3},{8,12},{9,13},{10,... | collective-permute-start | bytes 516104 | tf_op jit(solution)/shard_map/ppermute | solution.py:206
  107.8 9.9 %collective-permute-start.16 = (bf16[672,128]{1,0:T(8,128)(2,1)S(1)}, bf16[672,128]{1,0:T(8,128)(2,1)S(1)}, u32[]{:S(2)}, u32[]{:S(2)}) collective-permute-start(bf16[672,128]{1,0:T(8,128)(2,1)S(1)} %constant_dynamic-slice_fusion.1), channel_id=1, source_target_pairs={{0,2},{1,3},{2,0},{3,1},{4,6},{5,7},{6,4},{7,5},{8,10},{9,11},{10,... | collective-permute-start | bytes 516104 | tf_op jit(solution)/shard_map/ppermute | solution.py:199
  114.9 5.5 %copy-start = (bf16[128,1024]{1,0:T(8,128)(2,1)S(1)}, bf16[128,1024]{1,0:T(8,128)(2,1)}, u32[]{:S(2)}) copy-start(bf16[128,1024]{1,0:T(8,128)(2,1)} %trans_in.11) | copy-start | bytes 786436
  114.9 5.5 %copy-start.4 = (bf16[512,128]{1,0:T(8,128)(2,1)S(1)}, bf16[512,128]{1,0:T(8,128)(2,1)}, u32[]{:S(2)}) copy-start(bf16[512,128]{1,0:T(8,128)(2,1)} %trans_out.11) | copy-start | bytes 393220
  115.0 5.5 %copy-start.6 = (bf16[128,128]{1,0:T(8,128)(2,1)S(1)}, bf16[128,128]{1,0:T(8,128)(2,1)}, u32[]{:S(2)}) copy-start(bf16[128,128]{1,0:T(8,128)(2,1)} %w_out.11) | copy-start | bytes 98308
  115.0 5.5 %copy-start.11 = (f32[128]{0:T(128)S(1)}, f32[128]{0:T(128)}, u32[]{:S(2)}) copy-start(f32[128]{0:T(128)} %param.20) | copy-start | bytes 1540
  115.0 5.5 %copy-start.12 = (f32[128]{0:T(128)S(1)}, f32[128]{0:T(128)}, u32[]{:S(2)}) copy-start(f32[128]{0:T(128)} %param.23) | copy-start | bytes 1540
  115.0 17.5 %collective-permute-start.10 = (bf16[1344,128]{1,0:T(8,128)(2,1)S(1)}, bf16[1344,128]{1,0:T(8,128)(2,1)S(1)}, u32[]{:S(2)}, u32[]{:S(2)}) collective-permute-start(bf16[1344,128]{1,0:T(8,128)(2,1)S(1)} %constant_dynamic-slice_fusion.4), channel_id=1, source_target_pairs={{0,2},{1,3},{2,0},{3,1},{4,6},{5,7},{6,4},{7,5},{8,10},{9,11},{10,... | collective-permute-start | bytes 1032200 | tf_op jit(solution)/shard_map/ppermute | solution.py:199
  117.8 13.9 %collective-permute-start.17 = (bf16[336,128]{1,0:T(8,128)(2,1)S(1)}, bf16[336,128]{1,0:T(8,128)(2,1)S(1)}, u32[]{:S(2)}, u32[]{:S(2)}) collective-permute-start(bf16[336,128]{1,0:T(8,128)(2,1)S(1)} %constant_dynamic-slice_fusion), channel_id=1, source_target_pairs={{0,4},{1,5},{2,6},{3,7},{4,0},{5,1},{6,2},{7,3},{8,12},{9,13},{10,... | collective-permute-start | bytes 258056 | tf_op jit(solution)/shard_map/ppermute | solution.py:199
  118.1 30.0 %collective-permute-start.23 = (bf16[1344,128]{1,0:T(8,128)(2,1)S(1)}, bf16[1344,128]{1,0:T(8,128)(2,1)S(1)}, u32[]{:S(2)}, u32[]{:S(2)}) collective-permute-start(bf16[1344,128]{1,0:T(8,128)(2,1)S(1)} %maximum_select_fusion.3), channel_id=1, source_target_pairs={{0,2},{1,3},{2,0},{3,1},{4,6},{5,7},{6,4},{7,5},{8,10},{9,11},{10,... | collective-permute-start | bytes 1032200 | tf_op jit(solution)/shard_map/ppermute | solution.py:206
  131.7 5.8 %collective-permute-start.18 = (bf16[336,128]{1,0:T(8,128)(2,1)S(1)}, bf16[336,128]{1,0:T(8,128)(2,1)S(1)}, u32[]{:S(2)}, u32[]{:S(2)}) collective-permute-start(bf16[336,128]{1,0:T(8,128)(2,1)S(1)} %add_convert_fusion.8), channel_id=1, source_target_pairs={{0,4},{1,5},{2,6},{3,7},{4,0},{5,1},{6,2},{7,3},{8,12},{9,13},{10,... | collective-permute-start | bytes 258056 | tf_op jit(solution)/shard_map/ppermute | solution.py:206
  132.7 13.2 %collective-permute-start.11 = (bf16[672,128]{1,0:T(8,128)(2,1)S(1)}, bf16[672,128]{1,0:T(8,128)(2,1)S(1)}, u32[]{:S(2)}, u32[]{:S(2)}) collective-permute-start(bf16[672,128]{1,0:T(8,128)(2,1)S(1)} %constant_dynamic-slice_fusion.3), channel_id=1, source_target_pairs={{0,4},{1,5},{2,6},{3,7},{4,0},{5,1},{6,2},{7,3},{8,12},{9,13},{10,... | collective-permute-start | bytes 516104 | tf_op jit(solution)/shard_map/ppermute | solution.py:199
  137.6 9.9 %collective-permute-start.19 = (bf16[672,128]{1,0:T(8,128)(2,1)S(1)}, bf16[672,128]{1,0:T(8,128)(2,1)S(1)}, u32[]{:S(2)}, u32[]{:S(2)}) collective-permute-start(bf16[672,128]{1,0:T(8,128)(2,1)S(1)} %maximum_select_fusion.6), channel_id=1, source_target_pairs={{0,2},{1,3},{2,0},{3,1},{4,6},{5,7},{6,4},{7,5},{8,10},{9,11},{10,... | collective-permute-start | bytes 516104 | tf_op jit(solution)/shard_map/ppermute | solution.py:206
  145.9 4.6 %collective-permute-start.12 = (bf16[336,128]{1,0:T(8,128)(2,1)S(1)}, bf16[336,128]{1,0:T(8,128)(2,1)S(1)}, u32[]{:S(2)}, u32[]{:S(2)}) collective-permute-start(bf16[336,128]{1,0:T(8,128)(2,1)S(1)} %constant_dynamic-slice_fusion.2), channel_id=1, source_target_pairs={{0,1},{1,0},{2,3},{3,2},{4,5},{5,4},{6,7},{7,6},{8,9},{9,8},{10,11... | collective-permute-start | bytes 258056 | tf_op jit(solution)/shard_map/ppermute | solution.py:199
  147.6 26.7 %collective-permute-start.20 = (bf16[1344,128]{1,0:T(8,128)(2,1)S(1)}, bf16[1344,128]{1,0:T(8,128)(2,1)S(1)}, u32[]{:S(2)}, u32[]{:S(2)}) collective-permute-start(bf16[1344,128]{1,0:T(8,128)(2,1)S(1)} %maximum_select_fusion.2), channel_id=1, source_target_pairs={{0,1},{1,0},{2,3},{3,2},{4,5},{5,4},{6,7},{7,6},{8,9},{9,8},{10,11... | collective-permute-start | bytes 1032200 | tf_op jit(solution)/shard_map/ppermute | solution.py:206
  150.5 12.8 %collective-permute-start.13 = (bf16[336,128]{1,0:T(8,128)(2,1)S(1)}, bf16[336,128]{1,0:T(8,128)(2,1)S(1)}, u32[]{:S(2)}, u32[]{:S(2)}) collective-permute-start(bf16[336,128]{1,0:T(8,128)(2,1)S(1)} %add_convert_fusion.9), channel_id=1, source_target_pairs={{0,1},{1,0},{2,3},{3,2},{4,5},{5,4},{6,7},{7,6},{8,9},{9,8},{10,11... | collective-permute-start | bytes 258056 | tf_op jit(solution)/shard_map/ppermute | solution.py:206
  163.3 10.7 %collective-permute-start.14 = (bf16[672,128]{1,0:T(8,128)(2,1)S(1)}, bf16[672,128]{1,0:T(8,128)(2,1)S(1)}, u32[]{:S(2)}, u32[]{:S(2)}) collective-permute-start(bf16[672,128]{1,0:T(8,128)(2,1)S(1)} %maximum_select_fusion.5), channel_id=1, source_target_pairs={{0,4},{1,5},{2,6},{3,7},{4,0},{5,1},{6,2},{7,3},{8,12},{9,13},{10,... | collective-permute-start | bytes 516104 | tf_op jit(solution)/shard_map/ppermute | solution.py:206
  174.2 17.7 %collective-permute-start.15 = (bf16[1344,128]{1,0:T(8,128)(2,1)S(1)}, bf16[1344,128]{1,0:T(8,128)(2,1)S(1)}, u32[]{:S(2)}, u32[]{:S(2)}) collective-permute-start(bf16[1344,128]{1,0:T(8,128)(2,1)S(1)} %maximum_select_fusion.1), channel_id=1, source_target_pairs={{0,2},{1,3},{2,0},{3,1},{4,6},{5,7},{6,4},{7,5},{8,10},{9,11},{10,... | collective-permute-start | bytes 1032200 | tf_op jit(solution)/shard_map/ppermute | solution.py:206
